TPU v7x, 128 devices: a whole 4x4x4 slice. The times are simulated.
128 devices in a mesh: dp: 16 (over y_hi, z, core), tensor: 8 (over y_lo, x).
Axes of the slice: x: 4, y: 4 (y_hi: 2, y_lo: 2; y = y_hi * 2 + y_lo), z: 4, core: 2. Of those that a mesh axis runs over, the one named last changes fastest.
Arguments:
- tokens: bfloat16 [2048, 8192], P('dp'), may hold values from -6 to 6
- target: bfloat16 [2048, 8192], P('dp'), may hold values from -6 to 6
- norm_gain: float32 [8192], replicated, may hold values from 0.1 to 1.9
- w_query: bfloat16 [8192, 4096], P(None, 'tensor'), may hold values from -0.0625 to 0.0625
- w_key: bfloat16 [8192, 1024], P(None, 'tensor'), may hold values from -0.0625 to 0.0625
- w_value: bfloat16 [8192, 1024], P(None, 'tensor'), may hold values from -0.0625 to 0.0625
- w_out: bfloat16 [4096, 8192], P('tensor'), may hold values from -0.09375 to 0.09375
- t_query: float32 [4096], P('tensor'), may hold values from -4 to 4
- t_key: float32 [1024], P('tensor'), may hold values from -4 to 4
- t_value: float32 [1024], P('tensor'), may hold values from -4 to 4
- t_out: float32 [8192], replicated, may hold values from -4 to 4
Outputs:
- hvp_query: float32 [8192, 4096], P('dp', 'tensor')
- hvp_key: float32 [8192, 1024], P('dp', 'tensor')
- hvp_value: float32 [8192, 1024], P('dp', 'tensor')
- hvp_out: float32 [8192, 4096], P('dp', 'tensor')
All inputs are finite; a program needn't handle non-finite values.
Results may differ from a plain program's by a relative error of at most 0.02.
Values may be sent and summed in bfloat16 or wider, within the bound.
A program may use at most 128 MiB of HBM per device.

v0:
```python
import math

import jax
import jax.numpy as jnp
from jax import lax
from jax.sharding import PartitionSpec as P

HD = 128


EPS = 1e-05


def rms_norm(row_block, norm_gain):
    widened = row_block.astype(jnp.float32)
    inv_rms = lax.rsqrt(jnp.mean(widened * widened, axis=1, keepdims=True) + EPS)
    return (widened * inv_rms * norm_gain).astype(jnp.bfloat16)


def rotary(vectors, head_size):
    length = vectors.shape[0]
    half_width = head_size // 2
    position = jnp.arange(length).astype(jnp.float32)
    frequency = jnp.exp(
        -math.log(10000.0) * jnp.arange(half_width).astype(jnp.float32) * 2.0 / head_size
    )
    angles = position[:, None] * frequency[None, :]
    bcast_shape = (length,) + (1,) * (vectors.ndim - 2) + (half_width,)
    cosine_table = jnp.cos(angles).reshape(bcast_shape)
    sine_table = jnp.sin(angles).reshape(bcast_shape)
    front_half = vectors[..., :half_width]
    back_half = vectors[..., half_width:]
    return jnp.concatenate(
        [
            front_half * cosine_table - back_half * sine_table,
            back_half * cosine_table + front_half * sine_table,
        ],
        -1,
    )


def attend(proj_query, proj_key, proj_value):
    length = proj_query.shape[0]
    kv_count = proj_key.shape[1] // HD
    group_size = proj_query.shape[1] // proj_key.shape[1]
    rot_query = rotary(proj_query.reshape(length, kv_count, group_size, HD), HD)
    rot_key = rotary(proj_key.reshape(length, kv_count, HD), HD)
    head_values = proj_value.reshape(length, kv_count, HD)
    scores = jnp.einsum(
        "skgd,tkd->kgst", rot_query, rot_key, precision=lax.Precision.HIGHEST
    ) / math.sqrt(HD)
    causal = jnp.arange(length)[:, None] >= jnp.arange(length)[None, :]
    scores = jnp.where(causal, scores, -1e30)
    attn_probs = jax.nn.softmax(scores, axis=-1)
    mixed_heads = jnp.einsum(
        "kgst,tkd->skgd", attn_probs, head_values, precision=lax.Precision.HIGHEST
    )
    return mixed_heads.reshape(length, kv_count * group_size * HD)


def pullback(proj_query, proj_key, proj_value, cotangent):
    return jax.vjp(attend, proj_query, proj_key, proj_value)[1](cotangent)


def local_forward(
    normed,
    slice_query,
    slice_key,
    slice_value,
    slice_out,
    scale_query,
    scale_key,
    scale_value,
    t_out,
):
    proj_query = jnp.dot(normed, slice_query, preferred_element_type=jnp.float32)
    proj_key = jnp.dot(normed, slice_key, preferred_element_type=jnp.float32)
    proj_value = jnp.dot(normed, slice_value, preferred_element_type=jnp.float32)
    tan_query = proj_query * scale_query
    tan_key = proj_key * scale_key
    tan_value = proj_value * scale_value
    attn, tan_attn = jax.jvp(
        attend, (proj_query, proj_key, proj_value), (tan_query, tan_key, tan_value)
    )
    attn_low = attn.astype(jnp.bfloat16)
    tan_attn_low = tan_attn.astype(jnp.bfloat16)
    length = normed.shape[0]
    products = jnp.dot(
        jnp.concatenate([attn_low, tan_attn_low], 0), slice_out, preferred_element_type=jnp.float32
    )
    part_rows = products[:length]
    tan_part = products[length:] + part_rows * t_out
    return (
        proj_query,
        proj_key,
        proj_value,
        tan_query,
        tan_key,
        tan_value,
        attn_low,
        tan_attn_low,
        part_rows,
        tan_part,
    )


def local_grad(residual, tan_residual, slice_out, t_out, forward_vals):
    length = residual.shape[0]
    back_tan = (tan_residual.astype(jnp.float32) + residual.astype(jnp.float32) * t_out).astype(
        jnp.bfloat16
    )
    back_lhs = jnp.concatenate([residual, back_tan], 0)
    back_rows = lax.dot_general(
        back_lhs, slice_out, (((1,), (1,)), ((), ())), preferred_element_type=jnp.float32
    )
    primals = (forward_vals[0], forward_vals[1], forward_vals[2], back_rows[:length])
    tangents = (forward_vals[3], forward_vals[4], forward_vals[5], back_rows[length:])
    unused, grad_tans = jax.jvp(pullback, primals, tangents)
    return jnp.concatenate(list(grad_tans), 1).astype(jnp.bfloat16)


def local(
    tokens, target, norm_gain, w_query, w_key, w_value, w_out, t_query, t_key, t_value, t_out
):
    normed = rms_norm(tokens, norm_gain)
    forward_vals = local_forward(
        normed, w_query, w_key, w_value, w_out, t_query, t_key, t_value, t_out
    )
    sum_total, tan_total = (
        lax.psum(forward_vals[8].astype(jnp.bfloat16), "tensor").astype(jnp.float32),
        lax.psum(forward_vals[9].astype(jnp.bfloat16), "tensor").astype(jnp.float32),
    )
    residual = (tokens.astype(jnp.float32) + sum_total - target.astype(jnp.float32)).astype(
        jnp.bfloat16
    )
    tan_residual = tan_total.astype(jnp.bfloat16)
    grad_tangent = local_grad(residual, tan_residual, w_out, t_out, forward_vals)
    q_width = w_query.shape[1]
    k_width = w_key.shape[1]
    in_term = lax.dot_general(
        normed, grad_tangent, (((0,), (0,)), ((), ())), preferred_element_type=jnp.float32
    )
    resid_pair = jnp.concatenate([tan_residual, residual], 0)
    attn_pair = jnp.concatenate([forward_vals[6], forward_vals[7]], 0)
    out_term = lax.dot_general(
        resid_pair, attn_pair, (((0,), (0,)), ((), ())), preferred_element_type=jnp.float32
    )
    in_sum, out_sum = (
        lax.psum_scatter(
            in_term.astype(jnp.bfloat16), "dp", scatter_dimension=0, tiled=True
        ).astype(jnp.float32),
        lax.psum_scatter(
            out_term.astype(jnp.bfloat16), "dp", scatter_dimension=0, tiled=True
        ).astype(jnp.float32),
    )
    hvp_query = in_sum[:, :q_width]
    hvp_key = in_sum[:, q_width : q_width + k_width]
    hvp_value = in_sum[:, q_width + k_width :]
    return (hvp_query, hvp_key, hvp_value, out_sum)


def solution(mesh):
    return jax.shard_map(
        local,
        mesh=mesh,
        in_specs=(
            P("dp", None),
            P("dp", None),
            P(),
            P(None, "tensor"),
            P(None, "tensor"),
            P(None, "tensor"),
            P("tensor", None),
            P("tensor"),
            P("tensor"),
            P("tensor"),
            P(),
        ),
        out_specs=(P("dp", "tensor"), P("dp", "tensor"), P("dp", "tensor"), P("dp", "tensor")),
        check_vma=False,
    )
```

profile of v0, /device:TPU:13, one launch (start us, length us, event | category | flops | bytes accessed | tf_op | source)
XLA Modules:
  0.0 387.5 jit_solution(2652557995405112608)
XLA Ops:
  7.3 2.2 fusion
  9.6 3.2 fusion.104
  12.8 2.7 fusion.102
  15.5 1.3 broadcast_multiply_fusion
  22.1 5.9 %fusion.50 = f32[256,8192]{1,0:T(8,128)S(1)} fusion(bf16[512,8192]{1,0:T(8,128)(2,1)} %param.17, bf16[128,512]{0,1:T(8,128)(2,1)S(1)} %bitcast.201, bf16[128,512]{0,1:T(8,128)(2,1)S(1)} %bitcast.199), kind=kOutput, calls=%fused_computation.87 | convolution fusion | flops 2148007936 | bytes 17039360 | tf_op jit(solution)/shard_map/dot_general | solution.py:88
  28.0 1.6 slice.96
  29.6 1.9 fusion.5
  31.8 105.4 %all-reduce.7.cloned.1.call-done = (bf16[128,8192]{1,0:T(8,128)(2,1)}, bf16[128,8192]{1,0:T(8,128)(2,1)}) async-done(((bf16[128,8192]{1,0:T(8,128)(2,1)}, bf16[128,8192]{1,0:T(8,128)(2,1)}), (bf16[128,8192]{1,0:T(8,128)(2,1)}, bf16[128,8192]{1,0:T(8,128)(2,1)})) %all-reduce.7.cloned.1.call-update) | async-done | bytes 4194320 | tf_op jit(solution)/shard_map/psum | solution.py:130
  137.2 5.8 %add_convert_fusion = (bf16[128,8192]{1,0:T(8,128)(2,1)}, bf16[128,8192]{1,0:T(8,128)(2,1)S(1)}) fusion(bf16[128,8192]{1,0:T(8,128)(2,1)} %get-tuple-element.7, f32[8192]{0:T(1024)} %param.21, bf16[128,8192]{1,0:T(8,128)(2,1)} %param.12, bf16[128,8192]{1,0:T(8,128)(2,1)} %get-tuple-element.6, bf16[128,8192]{1,0:T(8,128)(2,1)S(1)} %copy-done.3), kind=kLoop, calls=%fused_computation.19 | loop fusion | flops 11534336 | bytes 12615680 | tf_op jit(solution)/shard_map/convert_element_type | solution.py:109
  143.0 1.4 copy-done.6
  144.4 4.7 %convolution_convert_fusion.1 = bf16[8192,512]{1,0:T(8,128)(2,1)} fusion(bf16[128,8192]{1,0:T(8,128)(2,1)S(1)} %get-tuple-element.9, bf16[128,8192]{1,0:T(8,128)(2,1)S(1)} %copy-done.5, bf16[128,512]{0,1:T(8,128)(2,1)S(1)} %bitcast.202, bf16[128,512]{0,1:T(8,128)(2,1)S(1)} %bitcast.200), kind=kOutput, calls=%fused_computation.1 | convolution fusion | flops 2160590848 | bytes 12845056 | tf_op jit(solution)/shard_map/dot_general | solution.py:145
  149.2 7.0 %fusion.6 = f32[256,512]{1,0:T(8,128)S(1)} fusion(bf16[512,8192]{1,0:T(8,128)(2,1)} %param.17, bf16[128,8192]{1,0:T(8,128)(2,1)} %get-tuple-element.8, bf16[128,8192]{1,0:T(8,128)(2,1)} %copy-done.6), kind=kOutput, calls=%fused_computation.12 | convolution fusion | flops 2155872256 | bytes 13107200 | tf_op jit(solution)/shard_map/dot_general | solution.py:113
  158.9 1.4 fusion.55
  160.3 1.2 convolution_add_fusion.1
  161.5 1.3 fusion.37
  167.4 1.9 convolution_bitcast_fusion.2
  170.9 1.5 convolution_bitcast_fusion
  172.4 1.4 fusion.25
  173.8 6.5 %convolution_convert_fusion = bf16[8192,768]{1,0:T(8,128)(2,1)} fusion(bf16[128,128]{0,1:T(8,128)(2,1)S(1)} %fusion.25, bf16[128,128]{0,1:T(8,128)(2,1)S(1)} %fusion.81, bf16[128,512]{0,1:T(8,128)(2,1)S(1)} %bitcast.197, bf16[128,8192]{1,0:T(8,128)(2,1)S(1)} %copy-done.3, f32[8192]{0:T(1024)S(1)} %copy-done.25, f32[128]{0:T(128)S(1)} %copy-done.36), kind=kOutput, calls=%fused_computation | convolution fusion | flops 1621688320 | bytes 14909952 | tf_op jit(solution)/shard_map/dot_general | solution.py:140
  180.3 70.8 %reduce-scatter.5.cloned.1.call-done = bf16[512,512]{1,0:T(8,128)(2,1)} async-done(((bf16[8192,512]{1,0:T(8,128)(2,1)}), bf16[512,512]{1,0:T(8,128)(2,1)}) %reduce-scatter.5.cloned.1.call-update) | async-done | bytes 524304 | tf_op jit(solution)/shard_map/reduce_scatter | solution.py:152
  251.2 2.1 convert_element_type.205
  253.3 123.8 %reduce-scatter.3.cloned.1.call-done = bf16[512,768]{1,0:T(8,128)(2,1)} async-done(((bf16[8192,768]{1,0:T(8,128)(2,1)}), bf16[512,768]{1,0:T(8,128)(2,1)}) %reduce-scatter.3.cloned.1.call-update) | async-done | bytes 786448 | tf_op jit(solution)/shard_map/reduce_scatter | solution.py:149
  377.1 1.8 fusion.107
  378.9 2.1 slice.80
  (120 shorter events, 14.0 us)
Async XLA Ops:
  7.2 130.0 %all-reduce.7.cloned.1.call-start = ((), (), s32[]{:S(2)}) async-start(), calls=%async_computation.4 | async-start | bytes 8388608 | tf_op jit(solution)/shard_map/psum | solution.py:130
  7.3 10.2 %copy-start.33 = (f32[128]{0:T(128)}, f32[128]{0:T(128)S(1)}, u32[]{:S(2)}) copy-start(f32[128]{0:T(128)S(1)} %iota_convert_fusion) | copy-start | bytes 1540
  7.3 10.2 %copy-start.34 = (f32[64]{0:T(128)}, f32[64]{0:T(128)S(1)}, u32[]{:S(2)}) copy-start(f32[64]{0:T(128)S(1)} %multiply_exponential_fusion) | copy-start | bytes 772
  9.6 5.9 %copy-start.35 = (f32[128]{0:T(128)}, f32[128]{0:T(128)S(1)}, u32[]{:S(2)}) copy-start(f32[128]{0:T(128)S(1)} %add_rsqrt_fusion) | copy-start | bytes 1540
  9.6 5.9 %copy-start.39 = (bf16[8192,512]{1,0:T(8,128)(2,1)S(1)}, bf16[8192,512]{1,0:T(8,128)(2,1)}, u32[]{:S(2)}) copy-start(bf16[8192,512]{1,0:T(8,128)(2,1)} %param.14) | copy-start | bytes 25165828
  9.6 5.9 %copy-start.40 = (f32[512]{0:T(512)S(1)}, f32[512]{0:T(512)}, u32[]{:S(2)}) copy-start(f32[512]{0:T(512)} %param.18) | copy-start | bytes 6148
  18.2 9.7 %copy-start.7 = (f32[128,1,4,64]{3,0,2,1:T(8,128)}, f32[128,1,4,64]{3,0,2,1:T(8,128)S(1)}, u32[]{:S(2)}) copy-start(f32[128,1,4,64]{3,0,2,1:T(8,128)S(1)} %get-tuple-element.12) | copy-start | bytes 393220
  18.3 9.7 %copy-start.8 = (f32[128,1,4,64]{3,0,2,1:T(8,128)}, f32[128,1,4,64]{3,0,2,1:T(8,128)S(1)}, u32[]{:S(2)}) copy-start(f32[128,1,4,64]{3,0,2,1:T(8,128)S(1)} %get-tuple-element.13) | copy-start | bytes 393220
  20.0 141.6 %copy-start.4 = (f32[1,4,128,128]{2,3,1,0:T(8,128)}, f32[1,4,128,128]{2,3,1,0:T(8,128)S(1)}, u32[]{:S(2)}) copy-start(f32[1,4,128,128]{2,3,1,0:T(8,128)S(1)} %get-tuple-element.44) | copy-start | bytes 786436
  21.1 6.9 %copy-start.15 = (bf16[128,4,128]{2,0,1:T(8,128)(2,1)}, bf16[128,4,128]{2,0,1:T(8,128)(2,1)S(1)}, u32[]{:S(2)}) copy-start(bf16[128,4,128]{2,0,1:T(8,128)(2,1)S(1)} %convolution_convert_fusion.2) | copy-start | bytes 393220
  22.0 6.0 %copy-start.17 = (bf16[128,4,128]{2,0,1:T(8,128)(2,1)}, bf16[128,4,128]{2,0,1:T(8,128)(2,1)S(1)}, u32[]{:S(2)}) copy-start(bf16[128,4,128]{2,0,1:T(8,128)(2,1)S(1)} %fusion.17) | copy-start | bytes 393220
  31.5 105.7 %copy-start.3 = (bf16[128,8192]{1,0:T(8,128)(2,1)S(1)}, bf16[128,8192]{1,0:T(8,128)(2,1)}, u32[]{:S(2)}) copy-start(bf16[128,8192]{1,0:T(8,128)(2,1)} %param.11) | copy-start | bytes 6291460
  31.6 219.6 %reduce-scatter.5.cloned.1.call-start = ((), (), s32[]{:S(2)}) async-start(), calls=%async_computation.3 | async-start | bytes 8912896 | tf_op jit(solution)/shard_map/reduce_scatter | solution.py:152
  137.2 7.2 %copy-start.5 = (bf16[128,8192]{1,0:T(8,128)(2,1)S(1)}, bf16[128,8192]{1,0:T(8,128)(2,1)}, u32[]{:S(2)}) copy-start(bf16[128,8192]{1,0:T(8,128)(2,1)} %get-tuple-element.7) | copy-start | bytes 6291460
  137.2 7.2 %copy-start.16 = (bf16[128,4,128]{2,0,1:T(8,128)(2,1)S(1)}, bf16[128,4,128]{2,0,1:T(8,128)(2,1)}, u32[]{:S(2)}) copy-start(bf16[128,4,128]{2,0,1:T(8,128)(2,1)} %copy-done.15) | copy-start | bytes 393220
  137.2 7.2 %copy-start.18 = (bf16[128,4,128]{2,0,1:T(8,128)(2,1)S(1)}, bf16[128,4,128]{2,0,1:T(8,128)(2,1)}, u32[]{:S(2)}) copy-start(bf16[128,4,128]{2,0,1:T(8,128)(2,1)} %copy-done.17) | copy-start | bytes 393220
  149.1 228.0 %reduce-scatter.3.cloned.1.call-start = ((), (), s32[]{:S(2)}) async-start(), calls=%async_computation.2 | async-start | bytes 13369344 | tf_op jit(solution)/shard_map/reduce_scatter | solution.py:149
  158.9 5.9 %copy-start.21 = (f32[128,1,64]{0,2,1:T(8,128)S(1)}, f32[128,1,64]{0,2,1:T(8,128)}, u32[]{:S(2)}) copy-start(f32[128,1,64]{0,2,1:T(8,128)} %copy-done.20) | copy-start | bytes 98308
  158.9 5.9 %copy-start.23 = (f32[128,1,64]{0,2,1:T(8,128)S(1)}, f32[128,1,64]{0,2,1:T(8,128)}, u32[]{:S(2)}) copy-start(f32[128,1,64]{0,2,1:T(8,128)} %copy-done.22) | copy-start | bytes 98308
  158.9 5.9 %copy-start.27 = (f32[4,128]{1,0:T(4,128)S(1)}, f32[4,128]{1,0:T(4,128)}, u32[]{:S(2)}) copy-start(f32[4,128]{1,0:T(4,128)} %copy-done.26) | copy-start | bytes 6148
  158.9 5.9 %copy-start.29 = (f32[4,128]{1,0:T(4,128)S(1)}, f32[4,128]{1,0:T(4,128)}, u32[]{:S(2)}) copy-start(f32[4,128]{1,0:T(4,128)} %copy-done.28) | copy-start | bytes 6148
  167.4 6.4 %copy-start.25 = (f32[8192]{0:T(1024)S(1)}, f32[8192]{0:T(1024)}, u32[]{:S(2)}) copy-start(f32[8192]{0:T(1024)} %param.13) | copy-start | bytes 98308
  167.4 6.4 %copy-start.36 = (f32[128]{0:T(128)S(1)}, f32[128]{0:T(128)}, u32[]{:S(2)}) copy-start(f32[128]{0:T(128)} %copy-done.35) | copy-start | bytes 1540
  180.3 200.7 %copy-start.1 = (bf16[8192,128]{1,0:T(8,128)(2,1)S(1)}, bf16[8192,128]{1,0:T(8,128)(2,1)}, u32[]{:S(2)}) copy-start(bf16[8192,128]{1,0:T(8,128)(2,1)} %param.16) | copy-start | bytes 6291460
  (20 other events, 61.7 us)
Sparse Core Ops, SparseCore 0:
  31.7 105.4 all-reduce.6
  149.2 101.8 reduce-scatter.4
  255.5 121.5 reduce-scatter.2
where the time goes:
time: 390 us; the launch traced here: 388 us
  waiting for transfers between devices  300 us (77%)
  matrix products  44.7 us (11%)
  other arithmetic  16.6 us (4%)
  between operations  14.5 us (4%)
  local copies, waits for them, and re-layouts  11.3 us (3%)
    reduce_scatter x1, waiting for transfers between devices, local(): lax.psum_scatter(in_term.astype(jnp.bfloat16), 'dp', scatter_dimension=0,...  124 us
    psum x1, waiting for transfers between devices, local(): lax.psum(forward_vals[8].astype(jnp.bfloat16), 'tensor').astype(jnp.float32)  105 us
    reduce_scatter x1, waiting for transfers between devices, local(): lax.psum_scatter(out_term.astype(jnp.bfloat16), 'dp', scatter_dimension=0...  70.8 us
    dot_general x8, matrix products, attend(): jnp.einsum('kgst,tkd->skgd', attn_probs, head_values, precision=lax.Preci...  8.08 us
  transfers between devices with their start and end apart: 3, of which 3 were waited for; matrix products, arithmetic and copies ran while one was open for 9% of the time, Pallas kernels for 0%

commit v1 on v0

v1 whole, which is shorter than its diff:
```python
import functools
import math

import jax
import jax.numpy as jnp
import numpy as np
from jax import lax
from jax.experimental import pallas as pl
from jax.experimental.pallas import tpu as pltpu
from jax.sharding import PartitionSpec as P

HD = 128
HEADS = 4
SEQ = 128
D = 8192
QW = HEADS * HD
N_DP = 16
N_T = 8
C = 512
EPS = 1e-05
F32 = jnp.float32
BF16 = jnp.bfloat16
MESH = pl.DeviceIdType.MESH


def mm(a, b):
    return lax.dot_general(
        a.astype(BF16), b.astype(BF16), (((1,), (0,)), ((), ())), preferred_element_type=F32
    )


def mm_nt(a, b):
    return lax.dot_general(
        a.astype(BF16), b.astype(BF16), (((1,), (1,)), ((), ())), preferred_element_type=F32
    )


def mm_tn(a, b):
    return lax.dot_general(
        a.astype(BF16), b.astype(BF16), (((0,), (0,)), ((), ())), preferred_element_type=F32
    )


def mm_nt_wide(a, b):
    a_hi = a.astype(BF16)
    b_hi = b.astype(BF16)
    a_lo = (a - a_hi.astype(F32)).astype(BF16)
    b_lo = (b - b_hi.astype(F32)).astype(BF16)
    return mm_nt(a_hi, b_hi) + (mm_nt(a_hi, b_lo) + mm_nt(a_lo, b_hi))


def swap_halves(x):
    return jnp.concatenate([x[:, HD // 2 :], x[:, : HD // 2]], axis=1)


def stack_heads(x):
    return jnp.concatenate([x[:, h * HD : (h + 1) * HD] for h in range(HEADS)], axis=0)


def kernel(
    tok_hbm, tgt_hbm, gain, wq_hbm, wk_hbm, wv_hbm, wo_hbm, tq, tk, tv, t_out, cos_t, sin_t,
    hq, hk, hv, ho,
    tok, tgt, wq, wk, wv, wo, nrm, nrm_g, att_g, res_g, grd_g,
    pa, pb, ra1, rb1, ra2, rb2, r_a, r_b, g_acc, proj,
    prob, tprob, rot_q, kv, gbuf,
    in_sem, wqkv_sem, wo_sem,
    nrm_s, nrm_r, att_s, att_r, res_s, res_r, grd_s, grd_r,
    a1_s, a1_r, b1_s, b1_r, a2_s, a2_r, b2_s, b2_r,
    ax_s, ax_r, ay_s, ay_r, bx_s, bx_r, bf_s, bf_r, by_s, by_r,
):
    d = lax.axis_index("dp")
    t = lax.axis_index("tensor")
    x = lax.rem(t, 4)
    y = t // 4

    def at(dy, dx):
        return lax.rem(y + dy, 2) * 4 + lax.rem(x + dx, 4)

    def remote(src, dst, s_sem, r_sem, **where):
        return pltpu.make_async_remote_copy(
            src_ref=src, dst_ref=dst, send_sem=s_sem, recv_sem=r_sem,
            device_id=where, device_id_type=MESH,
        )

    tok_copy = pltpu.make_async_copy(tok_hbm, tok, in_sem.at[0])
    tok_copy.start()
    tgt_copy = pltpu.make_async_copy(
        tgt_hbm.at[:, pl.ds(pl.multiple_of(t * 2 * C, 2 * C), 2 * C)], tgt, in_sem.at[1]
    )

    def w_copies(c):
        rows = pl.ds(c * C, C)
        return (
            pltpu.make_async_copy(wq_hbm.at[rows, :], wq.at[c], wqkv_sem.at[0, c]),
            pltpu.make_async_copy(wk_hbm.at[rows, :], wk.at[c], wqkv_sem.at[1, c]),
            pltpu.make_async_copy(wv_hbm.at[rows, :], wv.at[c], wqkv_sem.at[2, c]),
        )

    def wo_copy(c):
        return pltpu.make_async_copy(
            wo_hbm.at[:, pl.ds(pl.multiple_of(c * C, C), C)], wo.at[c], wo_sem.at[c]
        )

    @pl.loop(0, N_DP)
    def _(c):
        for cp in w_copies(c):
            cp.start()

    tgt_copy.start()

    @pl.loop(0, N_DP)
    def _(c):
        wo_copy(c).start()

    bar = pltpu.get_barrier_semaphore()

    @pl.loop(1, N_DP)
    def _(r):
        pl.semaphore_signal(
            bar, inc=1, device_id={"dp": lax.rem(d + r, N_DP)}, device_id_type=MESH
        )

    for dy, dx in ((1, 0), (0, 1), (0, 2), (0, 3)):
        pl.semaphore_signal(bar, inc=1, device_id={"tensor": at(dy, dx)}, device_id_type=MESH)

    tok_copy.wait()

    def square_step(c, acc):
        v = tok[:, pl.ds(pl.multiple_of(c * C, C), C)].astype(F32)
        return acc + v * v

    squares = lax.fori_loop(0, N_DP, square_step, jnp.zeros((SEQ, C), F32))
    inv = lax.rsqrt(jnp.sum(squares, axis=1, keepdims=True) * (1.0 / D) + EPS)

    @pl.loop(0, N_DP)
    def _(c):
        cols = pl.ds(pl.multiple_of(c * C, C), C)
        nrm[c] = (tok[:, cols].astype(F32) * inv * gain[:, cols]).astype(BF16)

    nrm_g[d] = nrm[d]

    pl.semaphore_wait(bar, N_DP - 1 + 4)

    def nrm_copy(r):
        dest = lax.rem(d + r, N_DP)
        return remote(nrm.at[dest], nrm_g.at[d], nrm_s.at[r], nrm_r.at[d], dp=dest)

    @pl.loop(1, N_DP)
    def _(r):
        nrm_copy(r).start()

    proj[...] = jnp.zeros_like(proj)

    @pl.loop(0, N_DP)
    def _(c):
        for cp in w_copies(c):
            cp.wait()
        lhs = nrm[c]
        proj[:, :QW] += mm(lhs, wq[c])
        proj[:, QW : QW + HD] += mm(lhs, wk[c])
        proj[:, QW + HD :] += mm(lhs, wv[c])

    cos1 = cos_t[...]
    sin1 = sin_t[...]
    cos4 = jnp.concatenate([cos1] * HEADS, axis=0)
    sin4 = jnp.concatenate([sin1] * HEADS, axis=0)
    scale = 1.0 / math.sqrt(HD)

    q2 = proj[:, :QW]
    key = proj[:, QW : QW + HD]
    val = proj[:, QW + HD :]
    tval = val * tv[...]
    qs = stack_heads(q2)
    tqs = stack_heads(q2 * tq[...])
    rq = qs * cos4 + swap_halves(qs) * sin4
    trq = tqs * cos4 + swap_halves(tqs) * sin4
    tkey = key * tk[...]
    rk = key * cos1 + swap_halves(key) * sin1
    trk = tkey * cos1 + swap_halves(tkey) * sin1
    rot_q[...] = jnp.concatenate([rq.astype(BF16), trq.astype(BF16)], axis=0)
    kv[0] = rk.astype(BF16)
    kv[1] = trk.astype(BF16)
    kv[2] = val.astype(BF16)
    kv[3] = tval.astype(BF16)
    scores = mm_nt_wide(rq, rk) * scale
    tscores = (mm_nt_wide(trq, rk) + mm_nt_wide(rq, trk)) * scale
    row = lax.rem(lax.broadcasted_iota(jnp.int32, (HEADS * SEQ, SEQ), 0), SEQ)
    col = lax.broadcasted_iota(jnp.int32, (HEADS * SEQ, SEQ), 1)
    scores = jnp.where(row >= col, scores, -1e30)
    e = jnp.exp(scores - jnp.max(scores, axis=1, keepdims=True))
    p = e / jnp.sum(e, axis=1, keepdims=True)
    tp = p * (tscores - jnp.sum(p * tscores, axis=1, keepdims=True))
    prob[...] = p
    tprob[...] = tp
    o = mm(p, val)
    to = mm(tp, val) + mm(p, tval)
    for h in range(HEADS):
        att_g[d, :SEQ, h * HD : (h + 1) * HD] = to[h * SEQ : (h + 1) * SEQ].astype(BF16)
        att_g[d, SEQ:, h * HD : (h + 1) * HD] = o[h * SEQ : (h + 1) * SEQ].astype(BF16)

    def att_copy(r):
        return remote(
            att_g.at[d], att_g.at[d], att_s.at[r], att_r.at[d], dp=lax.rem(d + r, N_DP)
        )

    @pl.loop(1, N_DP)
    def _(r):
        att_copy(r).start()

    @pl.loop(0, N_DP)
    def _(c):
        wo_copy(c).wait()

    def t_cols(c):
        return t_out[:, pl.ds(pl.multiple_of(c * C, C), C)]

    def part(dy, dx, half, dst):
        c = at(dy, dx) * 2 + half
        rows = mm(att_g[d], wo[c])
        dst[dy, dx, :SEQ, :] = rows[SEQ:].astype(BF16)
        dst[dy, dx, SEQ:, :] = (rows[:SEQ] + rows[SEQ:] * t_cols(c)).astype(BF16)

    def a1_copy(dx):
        return remote(pa.at[1, dx], ra1.at[dx], a1_s.at[dx], a1_r.at[dx], tensor=at(1, 0))

    def b1_copy(dy, dx):
        return remote(
            pb.at[dy, dx], rb1.at[dy, dx], b1_s.at[dy, dx], b1_r.at[dy, dx], tensor=at(0, dx)
        )

    def a2_copy(dx):
        return remote(pa.at[0, dx], ra2.at[dx], a2_s.at[dx], a2_r.at[dx], tensor=at(0, dx))

    def b2_copy():
        return remote(pb.at[1, 0], rb2, b2_s, b2_r, tensor=at(1, 0))

    for dx in (1, 3, 2):
        part(1, dx, 0, pa)
        a1_copy(dx).start()
        part(1, dx, 1, pb)
        b1_copy(1, dx).start()
    part(1, 0, 0, pa)
    a1_copy(0).start()
    for dx in (1, 3, 2):
        part(0, dx, 1, pb)
        b1_copy(0, dx).start()
    part(1, 0, 1, pb)
    for dx in (1, 3, 2, 0):
        part(0, dx, 0, pa)
    part(0, 0, 1, pb)
    for dx in (1, 3, 2):
        a1_copy(dx).wait_recv()
        pa[0, dx] = (pa[0, dx].astype(F32) + ra1[dx].astype(F32)).astype(BF16)
        a2_copy(dx).start()
    total = pb[1, 0].astype(F32)
    for dx in (1, 3, 2):
        b1_copy(1, dx).wait_recv()
        total += rb1[1, dx].astype(F32)
    pb[1, 0] = total.astype(BF16)
    b2_copy().start()

    tgt_copy.wait()

    def residual(total, half, dst):
        c = t * 2 + half
        base = tok[:, pl.ds(pl.multiple_of(c * C, C), C)].astype(F32)
        aim = tgt[:, half * C : (half + 1) * C].astype(F32)
        dst[t, :SEQ, :] = (base + total[:SEQ] - aim).astype(BF16)
        dst[t, SEQ:, :] = total[SEQ:].astype(BF16)

    def ax_copy(dx, j):
        return remote(r_a.at[j], r_a.at[j], ax_s.at[dx], ax_r.at[dx], tensor=at(0, dx))

    def ay_copy(dx, j):
        return remote(r_a.at[j], r_a.at[j], ay_s.at[dx], ay_r.at[dx], tensor=at(1, 0))

    def bx_copy(dx, j):
        return remote(r_b.at[j], r_b.at[j], bx_s.at[dx], bx_r.at[dx], tensor=at(0, dx))

    def bf_copy(dx, j):
        return remote(r_b.at[j], r_b.at[j], bf_s.at[dx], bf_r.at[dx], tensor=at(0, dx))

    def by_copy(j):
        return remote(r_b.at[j], r_b.at[j], by_s, by_r, tensor=at(1, 0))

    def res_copy(j, half):
        src = (r_a, r_b)[half]
        c = 2 * j + half
        return remote(src.at[j], res_g.at[d], res_s.at[c], res_r.at[d], dp=c)

    def use(j, half):
        src = (r_a, r_b)[half]
        c = 2 * j + half

        @pl.when(c != d)
        def _():
            res_copy(j, half).start()

        @pl.when(c == d)
        def _():
            res_g[d] = src[j]

        rows = src[j]
        first = rows[:SEQ]
        second = (rows[SEQ:].astype(F32) + first.astype(F32) * t_cols(c)).astype(BF16)
        g_acc[...] += mm_nt(jnp.concatenate([first, second], axis=0), wo[c])

    a1_copy(0).wait_recv()
    total = pa[0, 0].astype(F32) + ra1[0].astype(F32)
    for dx in (1, 3, 2):
        a2_copy(dx).wait_recv()
        total += ra2[dx].astype(F32)
    residual(total, 0, r_a)
    for dx in (1, 3, 2):
        ax_copy(dx, t).start()
    ay_copy(0, t).start()

    total = pb[0, 0].astype(F32)
    for dx in (1, 3, 2):
        b1_copy(0, dx).wait_recv()
        total += rb1[0, dx].astype(F32)
    b2_copy().wait_recv()
    total += rb2[...].astype(F32)
    residual(total, 1, r_b)
    by_copy(t).start()
    for dx in (1, 3, 2):
        bx_copy(dx, t).start()

    g_acc[...] = jnp.zeros_like(g_acc)
    use(t, 0)
    use(t, 1)
    j = at(1, 0)
    by_copy(j).wait_recv()
    for dx in (1, 3, 2):
        bf_copy(dx, j).start()
    use(j, 1)
    for dx in (1, 3, 2):
        j = at(0, 4 - dx)
        ax_copy(dx, j).wait_recv()
        ay_copy(dx, j).start()
        use(j, 0)
    use_order = (1, 3, 2)
    j = at(1, 0)
    ay_copy(0, j).wait_recv()
    use(j, 0)
    for dx in use_order:
        j = at(0, 4 - dx)
        bx_copy(dx, j).wait_recv()
        use(j, 1)
    for dx in use_order:
        j = at(1, 4 - dx)
        ay_copy(dx, j).wait_recv()
        use(j, 0)
        bf_copy(dx, j).wait_recv()
        use(j, 1)

    key = kv[0]
    tkey = kv[1]
    val = kv[2]
    tval = kv[3]
    g1 = stack_heads(g_acc[:SEQ]).astype(BF16)
    g2 = stack_heads(g_acc[SEQ:]).astype(BF16)
    p = prob[...]
    tp = tprob[...]
    dpr = mm_nt(g1, val)
    tdpr = mm_nt(g2, val) + mm_nt(g1, tval)
    tval_grad = mm_tn(jnp.concatenate([tp, p], axis=0), jnp.concatenate([g1, g2], axis=0))
    grd_g[d, :, QW + HD :] = tval_grad.astype(BF16)
    dpr = dpr - jnp.sum(p * dpr, axis=1, keepdims=True)
    tdpr = tdpr - jnp.sum(tp * dpr + p * tdpr, axis=1, keepdims=True)
    ds = (p * dpr).astype(BF16)
    tds = (tp * dpr + p * tdpr).astype(BF16)
    both = jnp.concatenate([tds, ds], axis=0)
    trk_grad = mm_tn(both, rot_q[...]) * scale
    trk_grad = trk_grad * cos1 - swap_halves(trk_grad) * sin1
    grd_g[d, :, QW : QW + HD] = trk_grad.astype(BF16)
    trq_grad = (mm(tds, key) + mm(ds, tkey)) * scale
    trq_grad = trq_grad * cos4 - swap_halves(trq_grad) * sin4
    for h in range(HEADS):
        grd_g[d, :, h * HD : (h + 1) * HD] = trq_grad[h * SEQ : (h + 1) * SEQ].astype(BF16)

    def grd_copy(r):
        return remote(
            grd_g.at[d], grd_g.at[d], grd_s.at[r], grd_r.at[d], dp=lax.rem(d + r, N_DP)
        )

    @pl.loop(1, N_DP)
    def _(r):
        grd_copy(r).start()

    @pl.loop(1, N_DP)
    def _(r):
        src = lax.rem(d + N_DP - r, N_DP)
        remote(att_g.at[src], att_g.at[src], att_s.at[r], att_r.at[src], dp=src).wait_recv()

    @pl.loop(1, N_DP)
    def _(r):
        src = lax.rem(d + N_DP - r, N_DP)
        remote(res_g.at[src], res_g.at[src], res_s.at[r], res_r.at[src], dp=src).wait_recv()

    STEP = 4
    ho[...] = jnp.zeros_like(ho)

    @pl.loop(0, N_DP // STEP)
    def _(s):
        rows = pl.ds(s * STEP, STEP)
        lhs = res_g[rows].reshape(STEP * 2 * SEQ, C)
        rhs = att_g[rows].reshape(STEP * 2 * SEQ, QW)
        ho[...] += mm_tn(lhs, rhs)

    @pl.loop(1, N_DP)
    def _(r):
        src = lax.rem(d + N_DP - r, N_DP)
        remote(nrm_g.at[src], nrm_g.at[src], nrm_s.at[r], nrm_r.at[src], dp=src).wait_recv()

    @pl.loop(1, N_DP)
    def _(r):
        src = lax.rem(d + N_DP - r, N_DP)
        remote(grd_g.at[src], grd_g.at[src], grd_s.at[r], grd_r.at[src], dp=src).wait_recv()

    gbuf[...] = jnp.zeros_like(gbuf)

    @pl.loop(0, N_DP // STEP)
    def _(s):
        rows = pl.ds(s * STEP, STEP)
        lhs = nrm_g[rows].reshape(STEP * SEQ, C)
        rhs = grd_g[rows].reshape(STEP * SEQ, QW + 2 * HD)
        gbuf[...] += mm_tn(lhs, rhs)

    hq[...] = gbuf[:, :QW]
    hk[...] = gbuf[:, QW : QW + HD]
    hv[...] = gbuf[:, QW + HD :]

    @pl.loop(1, N_DP)
    def _(r):
        nrm_copy(r).wait_send()
        att_copy(r).wait_send()
        grd_copy(r).wait_send()

    @pl.loop(0, N_T)
    def _(j):
        for half in range(2):

            @pl.when(2 * j + half != d)
            def _():
                res_copy(j, half).wait_send()

    for dx in range(4):
        a1_copy(dx).wait_send()
        ay_copy(dx, t).wait_send()
    for dx in (1, 2, 3):
        b1_copy(0, dx).wait_send()
        b1_copy(1, dx).wait_send()
        a2_copy(dx).wait_send()
        ax_copy(dx, t).wait_send()
        bx_copy(dx, t).wait_send()
        bf_copy(dx, t).wait_send()
    b2_copy().wait_send()
    by_copy(t).wait_send()


def tables():
    frequency = np.exp(
        np.float32(-math.log(10000.0)) * np.arange(HD // 2, dtype=np.float32) * np.float32(2.0)
        / np.float32(HD)
    ).astype(np.float32)
    angles = np.arange(SEQ, dtype=np.float32)[:, None] * frequency[None, :]
    cosine = np.cos(angles).astype(np.float32)
    sine = np.sin(angles).astype(np.float32)
    return np.concatenate([cosine, cosine], 1), np.concatenate([-sine, sine], 1)


def local(
    tokens, target, norm_gain, w_query, w_key, w_value, w_out, t_query, t_key, t_value, t_out
):
    cos_t, sin_t = tables()
    any_spec = pl.BlockSpec(memory_space=pl.ANY)
    vmem = pl.BlockSpec(memory_space=pltpu.VMEM)
    dma = pltpu.SemaphoreType.DMA
    block = (2 * SEQ, C)
    scratch = [
        pltpu.VMEM((SEQ, D), BF16),
        pltpu.VMEM((SEQ, 2 * C), BF16),
        pltpu.VMEM((N_DP, C, QW), BF16),
        pltpu.VMEM((N_DP, C, HD), BF16),
        pltpu.VMEM((N_DP, C, HD), BF16),
        pltpu.VMEM((N_DP, QW, C), BF16),
        pltpu.VMEM((N_DP, SEQ, C), BF16),
        pltpu.VMEM((N_DP, SEQ, C), BF16),
        pltpu.VMEM((N_DP, 2 * SEQ, QW), BF16),
        pltpu.VMEM((N_DP,) + block, BF16),
        pltpu.VMEM((N_DP, SEQ, QW + 2 * HD), BF16),
        pltpu.VMEM((2, 4) + block, BF16),
        pltpu.VMEM((2, 4) + block, BF16),
        pltpu.VMEM((4,) + block, BF16),
        pltpu.VMEM((2, 4) + block, BF16),
        pltpu.VMEM((4,) + block, BF16),
        pltpu.VMEM(block, BF16),
        pltpu.VMEM((N_T,) + block, BF16),
        pltpu.VMEM((N_T,) + block, BF16),
        pltpu.VMEM((2 * SEQ, QW), F32),
        pltpu.VMEM((SEQ, QW + 2 * HD), F32),
        pltpu.VMEM((HEADS * SEQ, SEQ), F32),
        pltpu.VMEM((HEADS * SEQ, SEQ), F32),
        pltpu.VMEM((2 * HEADS * SEQ, HD), BF16),
        pltpu.VMEM((4, SEQ, HD), BF16),
        pltpu.VMEM((C, QW + 2 * HD), F32),
        dma((2,)), dma((3, N_DP)), dma((N_DP,)),
        dma((N_DP,)), dma((N_DP,)), dma((N_DP,)), dma((N_DP,)),
        dma((N_DP,)), dma((N_DP,)), dma((N_DP,)), dma((N_DP,)),
        dma((4,)), dma((4,)), dma((2, 4)), dma((2, 4)), dma((4,)), dma((4,)), dma, dma,
        dma((4,)), dma((4,)), dma((4,)), dma((4,)),
        dma((4,)), dma((4,)), dma((4,)), dma((4,)), dma, dma,
    ]
    return pl.pallas_call(
        kernel,
        out_shape=(
            jax.ShapeDtypeStruct((C, QW), F32),
            jax.ShapeDtypeStruct((C, HD), F32),
            jax.ShapeDtypeStruct((C, HD), F32),
            jax.ShapeDtypeStruct((C, QW), F32),
        ),
        in_specs=[
            any_spec, any_spec, vmem, any_spec, any_spec, any_spec, any_spec,
            vmem, vmem, vmem, vmem, vmem, vmem,
        ],
        out_specs=(vmem, vmem, vmem, vmem),
        scratch_shapes=scratch,
        compiler_params=pltpu.CompilerParams(
            collective_id=0, has_side_effects=True, vmem_limit_bytes=62 * 1024 * 1024
        ),
        cost_estimate=pl.CostEstimate(
            flops=10_000_000_000, bytes_accessed=26_000_000, transcendentals=65536
        ),
        name="hvp",
    )(
        tokens, target, norm_gain.reshape(1, D), w_query, w_key, w_value, w_out,
        t_query.reshape(1, QW), t_key.reshape(1, HD), t_value.reshape(1, HD),
        t_out.reshape(1, D), jnp.asarray(cos_t), jnp.asarray(sin_t),
    )


def solution(mesh):
    return jax.shard_map(
        local,
        mesh=mesh,
        in_specs=(
            P("dp", None),
            P("dp", None),
            P(),
            P(None, "tensor"),
            P(None, "tensor"),
            P(None, "tensor"),
            P("tensor", None),
            P("tensor"),
            P("tensor"),
            P("tensor"),
            P(),
        ),
        out_specs=(P("dp", "tensor"), P("dp", "tensor"), P("dp", "tensor"), P("dp", "tensor")),
        check_vma=False,
    )
```

time: 390 us -> 268 us (0.69)
  the two profiles are of different devices: /device:TPU:13 before, /device:TPU:117 now
where the time goes in v1:
time: 268 us
  Pallas kernels  262 us (98%)
  local copies, waits for them, and re-layouts  4.76 us (2%)
    pallas_call x1, Pallas kernels, local(): pl.pallas_call(kernel, out_shape=(jax.ShapeDtypeStruct((C, QW), F32), jax...  262 us

profile of v1, /device:TPU:117, one launch (start us, length us, event | category | flops | bytes accessed | tf_op | source)
XLA Modules:
  0.0 267.9 jit_solution(17333972005903323915)
XLA Ops:
  0.6 262.5 %hvp.1 = (f32[512,512]{1,0:T(8,128)}, f32[512,128]{1,0:T(8,128)}, f32[512,128]{1,0:T(8,128)}, f32[512,512]{1,0:T(8,128)}) custom-call(bf16[128,8192]{1,0:T(8,128)(2,1)} %tok_hbm.1, bf16[128,8192]{1,0:T(8,128)(2,1)} %tgt_hbm.1, f32[1,8192]{1,0:T(1,128)} %bitcast.5, bf16[8192,512]{1,0:T(8,128)(2,1)} %wq_hbm.1, bf16[8192,128]{1,0:T(8,128)(2,1)} %wk_hbm.1, ...), custom_call_target="tpu_custom_call" | custom-call | flops 10000000000 | bytes 26000000 | tf_op jit(solution)/shard_map/hvp/pallas_call | solution.py:515
  263.1 0.0 copy-start.2
  263.1 0.0 copy-start.1
  263.1 0.0 copy-start
  263.2 2.4 copy.21
  265.5 0.0 copy-done.2
  265.5 0.7 copy.22
  266.2 0.0 copy-done.1
  266.2 0.7 copy.23
  266.9 0.0 copy-done
  266.9 1.0 copy.24
Async XLA Ops:
  263.1 2.4 copy-start.2
  263.1 3.1 %copy-start.1 = (f32[512,128]{1,0:T(8,128)S(1)}, f32[512,128]{1,0:T(8,128)}, u32[]{:S(2)}) copy-start(f32[512,128]{1,0:T(8,128)} %get-tuple-element.10) | copy-start | bytes 786436
  263.1 3.8 %copy-start = (f32[512,512]{1,0:T(8,128)S(1)}, f32[512,512]{1,0:T(8,128)}, u32[]{:S(2)}) copy-start(f32[512,512]{1,0:T(8,128)} %get-tuple-element.11) | copy-start | bytes 3145732

commit v2 on v1

--- a/solution.py
+++ b/solution.py
@@ -60,11 +60,12 @@
 def kernel(
     tok_hbm, tgt_hbm, gain, wq_hbm, wk_hbm, wv_hbm, wo_hbm, tq, tk, tv, t_out, cos_t, sin_t,
     hq, hk, hv, ho,
-    tok, tgt, wq, wk, wv, wo, nrm, nrm_g, att_g, res_g, grd_g,
+    tok, tgt, wq, wk, wv, wo, nrm, nrm_g, att, sib, zr, yr, grd_g,
     pa, pb, ra1, rb1, ra2, rb2, r_a, r_b, g_acc, proj,
-    prob, tprob, rot_q, kv, gbuf,
+    prob, tprob, rot_q, kv,
     in_sem, wqkv_sem, wo_sem,
-    nrm_s, nrm_r, att_s, att_r, res_s, res_r, grd_s, grd_r,
+    nrm_s, nrm_r, sib_s, sib_r, z_s, z_r, y_s, y_r,
+    gz_s, gz_r, gy_s, gy_r, gf_s, gf_r, gs_s, gs_r,
     a1_s, a1_r, b1_s, b1_r, a2_s, a2_r, b2_s, b2_r,
     ax_s, ax_r, ay_s, ay_r, bx_s, bx_r, bf_s, bf_r, by_s, by_r,
 ):
@@ -72,6 +73,12 @@
     t = lax.axis_index("tensor")
     x = lax.rem(t, 4)
     y = t // 4
+    core = lax.rem(d, 2)
+    z = lax.rem(d // 2, 4)
+    y_hi = d // 8
+
+    def dev(ry, rz, rc):
+        return (lax.rem(y_hi + ry, 2) * 4 + lax.rem(z + rz, 4)) * 2 + lax.rem(core + rc, 2)
 
     def at(dy, dx):
         return lax.rem(y + dy, 2) * 4 + lax.rem(x + dx, 4)
@@ -141,13 +148,16 @@
 
     pl.semaphore_wait(bar, N_DP - 1 + 4)
 
-    def nrm_copy(r):
-        dest = lax.rem(d + r, N_DP)
-        return remote(nrm.at[dest], nrm_g.at[d], nrm_s.at[r], nrm_r.at[d], dp=dest)
-
-    @pl.loop(1, N_DP)
-    def _(r):
-        nrm_copy(r).start()
+    def nrm_copy(ry, rz, rc):
+        dest = dev(ry, rz, rc)
+        r = (ry * 4 + rz) * 2 + rc
+        return remote(nrm.at[dest], nrm_g.at[d], nrm_s.at[r], nrm_r.at[r], dp=dest)
+
+    early = [(0, rz, rc) for rz in (1, 3, 2) for rc in (0, 1)] + [(0, 0, 1)]
+    early += [(1, rz, rc) for rz in (0, 2) for rc in (0, 1)]
+    late = [(1, rz, rc) for rz in (1, 3) for rc in (0, 1)]
+    for rel in early:
+        nrm_copy(*rel).start()
 
     proj[...] = jnp.zeros_like(proj)
 
@@ -195,17 +205,8 @@
     o = mm(p, val)
     to = mm(tp, val) + mm(p, tval)
     for h in range(HEADS):
-        att_g[d, :SEQ, h * HD : (h + 1) * HD] = to[h * SEQ : (h + 1) * SEQ].astype(BF16)
-        att_g[d, SEQ:, h * HD : (h + 1) * HD] = o[h * SEQ : (h + 1) * SEQ].astype(BF16)
-
-    def att_copy(r):
-        return remote(
-            att_g.at[d], att_g.at[d], att_s.at[r], att_r.at[d], dp=lax.rem(d + r, N_DP)
-        )
-
-    @pl.loop(1, N_DP)
-    def _(r):
-        att_copy(r).start()
+        att[:SEQ, h * HD : (h + 1) * HD] = to[h * SEQ : (h + 1) * SEQ].astype(BF16)
+        att[SEQ:, h * HD : (h + 1) * HD] = o[h * SEQ : (h + 1) * SEQ].astype(BF16)
 
     @pl.loop(0, N_DP)
     def _(c):
@@ -216,7 +217,7 @@
 
     def part(dy, dx, half, dst):
         c = at(dy, dx) * 2 + half
-        rows = mm(att_g[d], wo[c])
+        rows = mm(att[...], wo[c])
         dst[dy, dx, :SEQ, :] = rows[SEQ:].astype(BF16)
         dst[dy, dx, SEQ:, :] = (rows[:SEQ] + rows[SEQ:] * t_cols(c)).astype(BF16)
 
@@ -283,27 +284,38 @@
     def by_copy(j):
         return remote(r_b.at[j], r_b.at[j], by_s, by_r, tensor=at(1, 0))
 
-    def res_copy(j, half):
-        src = (r_a, r_b)[half]
-        c = 2 * j + half
-        return remote(src.at[j], res_g.at[d], res_s.at[c], res_r.at[d], dp=c)
+    def sib_copy(j, half):
+        return remote(wq.at[half * N_T + j], sib.at[j], sib_s.at[j], sib_r.at[j], dp=dev(0, 0, 1))
 
     def use(j, half):
         src = (r_a, r_b)[half]
+        rows = src[j]
+        wq[half * N_T + j] = mm_tn(rows, att[...]).astype(BF16)
+
+        @pl.when(core != half)
+        def _():
+            sib_copy(j, half).start()
+
         c = 2 * j + half
-
-        @pl.when(c != d)
-        def _():
-            res_copy(j, half).start()
-
-        @pl.when(c == d)
-        def _():
-            res_g[d] = src[j]
-
-        rows = src[j]
         first = rows[:SEQ]
         second = (rows[SEQ:].astype(F32) + first.astype(F32) * t_cols(c)).astype(BF16)
         g_acc[...] += mm_nt(jnp.concatenate([first, second], axis=0), wo[c])
+
+    def z_copy(j):
+        slot = core * N_T + j
+        return remote(
+            wq.at[slot], zr.at[j // 4, z], z_s.at[j], z_r.at[j // 4, z],
+            dp=(y_hi * 4 + lax.rem(j, 4)) * 2 + core,
+        )
+
+    def combine(j):
+        slot = core * N_T + j
+        sib_copy(j, 0).wait_recv()
+        wq[slot] = (wq[slot].astype(F32) + sib[j].astype(F32)).astype(BF16)
+
+        @pl.when(lax.rem(j, 4) != z)
+        def _():
+            z_copy(j).start()
 
     a1_copy(0).wait_recv()
     total = pa[0, 0].astype(F32) + ra1[0].astype(F32)
@@ -334,25 +346,30 @@
     for dx in (1, 3, 2):
         bf_copy(dx, j).start()
     use(j, 1)
+    combine(t)
     for dx in (1, 3, 2):
         j = at(0, 4 - dx)
         ax_copy(dx, j).wait_recv()
         ay_copy(dx, j).start()
         use(j, 0)
-    use_order = (1, 3, 2)
     j = at(1, 0)
     ay_copy(0, j).wait_recv()
     use(j, 0)
-    for dx in use_order:
+    pending = [j]
+    for dx in (1, 3, 2):
         j = at(0, 4 - dx)
         bx_copy(dx, j).wait_recv()
         use(j, 1)
-    for dx in use_order:
+        combine(pending.pop())
+        pending.append(j)
+    for dx in (1, 3, 2):
         j = at(1, 4 - dx)
         ay_copy(dx, j).wait_recv()
         use(j, 0)
+        combine(pending.pop())
         bf_copy(dx, j).wait_recv()
         use(j, 1)
+        pending.append(j)
 
     key = kv[0]
     tkey = kv[1]
@@ -379,72 +396,100 @@
     for h in range(HEADS):
         grd_g[d, :, h * HD : (h + 1) * HD] = trq_grad[h * SEQ : (h + 1) * SEQ].astype(BF16)
 
-    def grd_copy(r):
+    def gs_copy(ry, rz):
+        b = dev(ry, 4 - rz, 0)
         return remote(
-            grd_g.at[d], grd_g.at[d], grd_s.at[r], grd_r.at[d], dp=lax.rem(d + r, N_DP)
+            grd_g.at[b], grd_g.at[b], gs_s.at[ry, rz], gs_r.at[ry, rz], dp=dev(0, 0, 1)
         )
 
-    @pl.loop(1, N_DP)
-    def _(r):
-        grd_copy(r).start()
-
-    @pl.loop(1, N_DP)
-    def _(r):
-        src = lax.rem(d + N_DP - r, N_DP)
-        remote(att_g.at[src], att_g.at[src], att_s.at[r], att_r.at[src], dp=src).wait_recv()
-
-    @pl.loop(1, N_DP)
-    def _(r):
-        src = lax.rem(d + N_DP - r, N_DP)
-        remote(res_g.at[src], res_g.at[src], res_s.at[r], res_r.at[src], dp=src).wait_recv()
+    def gz_copy(rz, b):
+        return remote(grd_g.at[b], grd_g.at[b], gz_s.at[rz], gz_r.at[rz], dp=dev(0, rz, 0))
+
+    def gf_copy(rz, b):
+        return remote(grd_g.at[b], grd_g.at[b], gf_s.at[rz], gf_r.at[rz], dp=dev(0, rz, 0))
+
+    def gy_copy(b):
+        return remote(grd_g.at[b], grd_g.at[b], gy_s, gy_r, dp=dev(1, 0, 0))
+
+    gy_copy(d).start()
+    for rz in (1, 3, 2):
+        gz_copy(rz, d).start()
+    gs_copy(0, 0).start()
+    combine(pending.pop())
+    for rel in late:
+        nrm_copy(*rel).start()
+    b = dev(1, 0, 0)
+    gy_copy(b).wait_recv()
+    for rz in (1, 3, 2):
+        gf_copy(rz, b).start()
+    gs_copy(1, 0).start()
+
+    def z_sum(yd):
+        total = wq[core * N_T + yd * 4 + z].astype(F32)
+        for rz in (1, 3, 2):
+            src = lax.rem(z + 4 - rz, 4)
+            remote(
+                zr.at[yd, src], zr.at[yd, src], z_s.at[0], z_r.at[yd, src], dp=dev(0, rz, 0)
+            ).wait_recv()
+            total += zr[yd, src].astype(F32)
+        return total
+
+    other = lax.rem(y_hi + 1, 2)
+    slot = core * N_T + other * 4 + z
+    wq[slot] = z_sum(other).astype(BF16)
+    y_copy = remote(wq.at[slot], yr, y_s, y_r, dp=dev(1, 0, 0))
+    y_copy.start()
+    ho[...] = z_sum(y_hi)
+
+    for rz in (1, 3, 2):
+        gz_copy(rz, dev(0, 4 - rz, 0)).wait_recv()
+        gs_copy(0, rz).start()
+    for rz in (1, 3, 2):
+        gf_copy(rz, dev(1, 4 - rz, 0)).wait_recv()
+        gs_copy(1, rz).start()
+    y_copy.wait_recv()
+    ho[...] += yr[...].astype(F32)
+
+    for ry, rz, rc in early + late:
+        src = dev(ry, 4 - rz, rc)
+        r = (ry * 4 + rz) * 2 + rc
+        remote(nrm_g.at[src], nrm_g.at[src], nrm_s.at[r], nrm_r.at[r], dp=src).wait_recv()
+    for ry in range(2):
+        for rz in range(4):
+            b = dev(ry, 4 - rz, 1)
+            remote(
+                grd_g.at[b], grd_g.at[b], gs_s.at[ry, rz], gs_r.at[ry, rz], dp=dev(0, 0, 1)
+            ).wait_recv()
 
     STEP = 4
-    ho[...] = jnp.zeros_like(ho)
-
-    @pl.loop(0, N_DP // STEP)
-    def _(s):
-        rows = pl.ds(s * STEP, STEP)
-        lhs = res_g[rows].reshape(STEP * 2 * SEQ, C)
-        rhs = att_g[rows].reshape(STEP * 2 * SEQ, QW)
-        ho[...] += mm_tn(lhs, rhs)
-
-    @pl.loop(1, N_DP)
-    def _(r):
-        src = lax.rem(d + N_DP - r, N_DP)
-        remote(nrm_g.at[src], nrm_g.at[src], nrm_s.at[r], nrm_r.at[src], dp=src).wait_recv()
-
-    @pl.loop(1, N_DP)
-    def _(r):
-        src = lax.rem(d + N_DP - r, N_DP)
-        remote(grd_g.at[src], grd_g.at[src], grd_s.at[r], grd_r.at[src], dp=src).wait_recv()
-
-    gbuf[...] = jnp.zeros_like(gbuf)
+    hq[...] = jnp.zeros_like(hq)
+    hk[...] = jnp.zeros_like(hk)
+    hv[...] = jnp.zeros_like(hv)
 
     @pl.loop(0, N_DP // STEP)
     def _(s):
         rows = pl.ds(s * STEP, STEP)
         lhs = nrm_g[rows].reshape(STEP * SEQ, C)
         rhs = grd_g[rows].reshape(STEP * SEQ, QW + 2 * HD)
-        gbuf[...] += mm_tn(lhs, rhs)
-
-    hq[...] = gbuf[:, :QW]
-    hk[...] = gbuf[:, QW : QW + HD]
-    hv[...] = gbuf[:, QW + HD :]
-
-    @pl.loop(1, N_DP)
-    def _(r):
-        nrm_copy(r).wait_send()
-        att_copy(r).wait_send()
-        grd_copy(r).wait_send()
+        out = mm_tn(lhs, rhs)
+        hq[...] += out[:, :QW]
+        hk[...] += out[:, QW : QW + HD]
+        hv[...] += out[:, QW + HD :]
+
+    for rel in early + late:
+        nrm_copy(*rel).wait_send()
 
     @pl.loop(0, N_T)
     def _(j):
-        for half in range(2):
-
-            @pl.when(2 * j + half != d)
-            def _():
-                res_copy(j, half).wait_send()
-
+        sib_copy(j, 0).wait_send()
+
+        @pl.when(lax.rem(j, 4) != z)
+        def _():
+            z_copy(j).wait_send()
+
+    for ry in range(2):
+        for rz in range(4):
+            gs_copy(ry, rz).wait_send()
     for dx in range(4):
         a1_copy(dx).wait_send()
         ay_copy(dx, t).wait_send()
@@ -455,6 +500,10 @@
         ax_copy(dx, t).wait_send()
         bx_copy(dx, t).wait_send()
         bf_copy(dx, t).wait_send()
+        gz_copy(dx, d).wait_send()
+        gf_copy(dx, d).wait_send()
+    gy_copy(d).wait_send()
+    y_copy.wait_send()
     b2_copy().wait_send()
     by_copy(t).wait_send()
 
@@ -487,8 +536,10 @@
         pltpu.VMEM((N_DP, QW, C), BF16),
         pltpu.VMEM((N_DP, SEQ, C), BF16),
         pltpu.VMEM((N_DP, SEQ, C), BF16),
-        pltpu.VMEM((N_DP, 2 * SEQ, QW), BF16),
-        pltpu.VMEM((N_DP,) + block, BF16),
+        pltpu.VMEM((2 * SEQ, QW), BF16),
+        pltpu.VMEM((N_T, C, QW), BF16),
+        pltpu.VMEM((2, 4, C, QW), BF16),
+        pltpu.VMEM((C, QW), BF16),
         pltpu.VMEM((N_DP, SEQ, QW + 2 * HD), BF16),
         pltpu.VMEM((2, 4) + block, BF16),
         pltpu.VMEM((2, 4) + block, BF16),
@@ -504,10 +555,9 @@
         pltpu.VMEM((HEADS * SEQ, SEQ), F32),
         pltpu.VMEM((2 * HEADS * SEQ, HD), BF16),
         pltpu.VMEM((4, SEQ, HD), BF16),
-        pltpu.VMEM((C, QW + 2 * HD), F32),
         dma((2,)), dma((3, N_DP)), dma((N_DP,)),
-        dma((N_DP,)), dma((N_DP,)), dma((N_DP,)), dma((N_DP,)),
-        dma((N_DP,)), dma((N_DP,)), dma((N_DP,)), dma((N_DP,)),
+        dma((N_DP,)), dma((N_DP,)), dma((N_T,)), dma((N_T,)), dma((N_T,)), dma((2, 4)), dma, dma,
+        dma((4,)), dma((4,)), dma, dma, dma((4,)), dma((4,)), dma((2, 4)), dma((2, 4)),
         dma((4,)), dma((4,)), dma((2, 4)), dma((2, 4)), dma((4,)), dma((4,)), dma, dma,
         dma((4,)), dma((4,)), dma((4,)), dma((4,)),
         dma((4,)), dma((4,)), dma((4,)), dma((4,)), dma, dma,

time: 268 us -> 169 us (0.63)
  the two profiles are of different devices: /device:TPU:117 before, /device:TPU:13 now
where the time goes in v2:
time: 169 us; the launch traced here: 167 us
  Pallas kernels  161 us (95%)
  local copies, waits for them, and re-layouts  4.76 us (3%)
    pallas_call x1, Pallas kernels, local(): pl.pallas_call(kernel, out_shape=(jax.ShapeDtypeStruct((C, QW), F32), jax...  161 us
    unnamed x10, local copies, waits for them, and re-layouts  4.76 us

profile of v2, /device:TPU:13, one launch (start us, length us, event | category | flops | bytes accessed | tf_op | source)
XLA Modules:
  0.0 166.7 jit_solution(4898625879669357271)
XLA Ops:
  0.6 161.3 %hvp.1 = (f32[512,512]{1,0:T(8,128)}, f32[512,128]{1,0:T(8,128)}, f32[512,128]{1,0:T(8,128)}, f32[512,512]{1,0:T(8,128)}) custom-call(bf16[128,8192]{1,0:T(8,128)(2,1)} %tok_hbm.1, bf16[128,8192]{1,0:T(8,128)(2,1)} %tgt_hbm.1, f32[1,8192]{1,0:T(1,128)} %bitcast.5, bf16[8192,512]{1,0:T(8,128)(2,1)} %wq_hbm.1, bf16[8192,128]{1,0:T(8,128)(2,1)} %wk_hbm.1, ...), custom_call_target="tpu_custom_call" | custom-call | flops 10000000000 | bytes 26000000 | tf_op jit(solution)/shard_map/hvp/pallas_call | solution.py:565
  161.9 0.0 copy-start.2
  161.9 0.0 copy-start.1
  161.9 0.0 copy-start
  161.9 2.4 %copy.21 = f32[512,512]{1,0:T(8,128)} copy(f32[512,512]{1,0:T(8,128)} %get-tuple-element.8) | data formatting | bytes 2097152
  164.3 0.0 copy-done.2
  164.3 0.7 copy.22
  165.0 0.0 copy-done.1
  165.0 0.7 copy.23
  165.7 0.0 copy-done
  165.7 1.0 copy.24
Async XLA Ops:
  161.9 2.4 %copy-start.2 = (f32[512,128]{1,0:T(8,128)S(1)}, f32[512,128]{1,0:T(8,128)}, u32[]{:S(2)}) copy-start(f32[512,128]{1,0:T(8,128)} %get-tuple-element.9) | copy-start | bytes 786436
  161.9 3.1 %copy-start.1 = (f32[512,128]{1,0:T(8,128)S(1)}, f32[512,128]{1,0:T(8,128)}, u32[]{:S(2)}) copy-start(f32[512,128]{1,0:T(8,128)} %get-tuple-element.10) | copy-start | bytes 786436
  161.9 3.8 %copy-start = (f32[512,512]{1,0:T(8,128)S(1)}, f32[512,512]{1,0:T(8,128)}, u32[]{:S(2)}) copy-start(f32[512,512]{1,0:T(8,128)} %get-tuple-element.11) | copy-start | bytes 3145732

commit v3 on v2

--- a/solution.py
+++ b/solution.py
@@ -60,14 +60,13 @@
 def kernel(
     tok_hbm, tgt_hbm, gain, wq_hbm, wk_hbm, wv_hbm, wo_hbm, tq, tk, tv, t_out, cos_t, sin_t,
     hq, hk, hv, ho,
-    tok, tgt, wq, wk, wv, wo, nrm, nrm_g, att, sib, zr, yr, grd_g,
-    pa, pb, ra1, rb1, ra2, rb2, r_a, r_b, g_acc, proj,
+    tok, tgt, wq, wk, wv, wo, nrm, nrm_g, att, sib, zf, zr, yr, grd_g,
+    pa, pb, f0, v0, c0, f1, v1, c1, f2, v2, c2, r_a, r_b, g_acc, proj,
     prob, tprob, rot_q, kv,
     in_sem, wqkv_sem, wo_sem,
     nrm_s, nrm_r, sib_s, sib_r, z_s, z_r, y_s, y_r,
-    gz_s, gz_r, gy_s, gy_r, gf_s, gf_r, gs_s, gs_r,
-    a1_s, a1_r, b1_s, b1_r, a2_s, a2_r, b2_s, b2_r,
-    ax_s, ax_r, ay_s, ay_r, bx_s, bx_r, bf_s, bf_r, by_s, by_r,
+    gz_s, gz_r, gy_s, gy_r, gs_s, gs_r,
+    s0_s, s0_r, s1_s, s1_r, s2_s, s2_r, g0_s, g0_r, g1_s, g1_r, g2_s, g2_r,
 ):
     d = lax.axis_index("dp")
     t = lax.axis_index("tensor")
@@ -154,10 +153,16 @@
         return remote(nrm.at[dest], nrm_g.at[d], nrm_s.at[r], nrm_r.at[r], dp=dest)
 
     early = [(0, rz, rc) for rz in (1, 3, 2) for rc in (0, 1)] + [(0, 0, 1)]
-    early += [(1, rz, rc) for rz in (0, 2) for rc in (0, 1)]
-    late = [(1, rz, rc) for rz in (1, 3) for rc in (0, 1)]
+    crossing = [[(1, rz, rc) for rc in (0, 1)] for rz in (2, 1, 3, 0)]
+    everyone = early + sum(crossing, [])
+
+    def nrm_cross(i):
+        for rel in crossing[i]:
+            nrm_copy(*rel).start()
+
     for rel in early:
         nrm_copy(*rel).start()
+    nrm_cross(0)
 
     proj[...] = jnp.zeros_like(proj)
 
@@ -221,44 +226,115 @@
         dst[dy, dx, :SEQ, :] = rows[SEQ:].astype(BF16)
         dst[dy, dx, SEQ:, :] = (rows[:SEQ] + rows[SEQ:] * t_cols(c)).astype(BF16)
 
-    def a1_copy(dx):
-        return remote(pa.at[1, dx], ra1.at[dx], a1_s.at[dx], a1_r.at[dx], tensor=at(1, 0))
-
-    def b1_copy(dy, dx):
-        return remote(
-            pb.at[dy, dx], rb1.at[dy, dx], b1_s.at[dy, dx], b1_r.at[dy, dx], tensor=at(0, dx)
-        )
-
-    def a2_copy(dx):
-        return remote(pa.at[0, dx], ra2.at[dx], a2_s.at[dx], a2_r.at[dx], tensor=at(0, dx))
-
-    def b2_copy():
-        return remote(pb.at[1, 0], rb2, b2_s, b2_r, tensor=at(1, 0))
-
-    for dx in (1, 3, 2):
+    class Stream:
+        def __init__(self, buf, r0, n, half_in, full_in, across, s, r, out, g_s, g_r):
+            self.buf, self.r0, self.n, self.h = buf, r0, n, n // 2
+            self.half_in, self.full_in, self.across = half_in, full_in, across
+            self.s, self.r, self.out, self.g_s, self.g_r = s, r, out, g_s, g_r
+
+        def ring(self, dy, k):
+            h = self.h
+            dx, upper, step = ((2, 0, 1), (2, 1, 3), (1, 1, 1), (3, 0, 3), (1, 0, 1), (3, 1, 3))[k]
+            src = self.buf.at[dy, dx, pl.ds(self.r0 + upper * h, h)]
+            side = 0 if step == 1 else 1
+            dst = self.half_in.at[dy, side] if k < 2 else self.full_in.at[dy, side, pl.ds(upper * h, h)]
+            return remote(src, dst, self.s.at[dy, k], self.r.at[dy, k], tensor=at(0, step))
+
+        def cross(self, dx):
+            rows = pl.ds(self.r0, self.n)
+            return remote(
+                self.buf.at[1, dx, rows], self.across.at[dx], self.s.at[2, dx], self.r.at[2, dx],
+                tensor=at(1, 0),
+            )
+
+        def add(self, dy, dx, upper, value):
+            lo = self.r0 + upper * self.h
+            rows = slice(lo, lo + value.shape[0])
+            self.buf[dy, dx, rows] = (self.buf[dy, dx, rows].astype(F32) + value.astype(F32)).astype(BF16)
+
+        def relay(self, dy):
+            self.ring(dy, 0).wait_recv()
+            self.add(dy, 1, 0, self.half_in[dy, 0])
+            self.ring(dy, 4).start()
+            self.ring(dy, 1).wait_recv()
+            self.add(dy, 3, 1, self.half_in[dy, 1])
+            self.ring(dy, 5).start()
+
+        def row_sum(self, dy):
+            for k in (2, 3, 4, 5):
+                self.ring(dy, k).wait_recv()
+            own = self.buf[dy, 0, self.r0 : self.r0 + self.n].astype(F32)
+            return own + self.full_in[dy, 0].astype(F32) + self.full_in[dy, 1].astype(F32)
+
+        def gather(self, k, sender=True):
+            sent = (t, t, t, at(0, 3), at(0, 1)) + (
+                (at(0, 3), at(0, 1), at(0, 2)) if self.r0 == 0 and self.n == SEQ
+                else (at(1, 0), at(1, 0), at(1, 3), at(1, 1))
+            )
+            came = (at(1, 0), at(0, 3), at(0, 1), at(0, 2), at(0, 2)) + (
+                (at(1, 3), at(1, 1), at(1, 2)) if self.r0 == 0 and self.n == SEQ
+                else (at(1, 3), at(1, 1), at(1, 2), at(1, 2))
+            )
+            first_y = not (self.r0 == 0 and self.n == SEQ)
+            to = (at(1, 0), at(0, 1), at(0, 3), at(0, 1), at(0, 3)) + (
+                (at(0, 1), at(0, 3), at(0, 1), at(0, 3)) if first_y else (at(1, 0),) * 3
+            )
+            j = sent[k] if sender else came[k]
+            lo, n = self.r0, self.n
+            if k == 3 or (k == 7 and first_y):
+                n = self.h
+            if k == 4 or (k == 8 and first_y):
+                lo, n = lo + self.h, self.h
+            ref = self.out.at[j, pl.ds(lo, n)]
+            return remote(ref, ref, self.g_s.at[k], self.g_r.at[k], tensor=to[k])
+
+        def came(self, *ks):
+            for k in ks:
+                self.gather(k, False).wait_recv()
+
+    s0 = Stream(pa, 0, SEQ, f0, v0, c0, s0_s, s0_r, r_a, g0_s, g0_r)
+    s1 = Stream(pa, SEQ, SEQ, f1, v1, c1, s1_s, s1_r, r_a, g1_s, g1_r)
+    s2 = Stream(pb, 0, 2 * SEQ, f2, v2, c2, s2_s, s2_r, r_b, g2_s, g2_r)
+    x_first = (s2, s1)
+
+    for dx, ks in ((2, (0, 1)), (1, (2,)), (3, (3,))):
+        part(1, dx, 1, pb)
+        for k in ks:
+            s2.ring(1, k).start()
         part(1, dx, 0, pa)
-        a1_copy(dx).start()
-        part(1, dx, 1, pb)
-        b1_copy(1, dx).start()
+        for k in ks:
+            s1.ring(1, k).start()
+        s0.cross(dx).start()
+    part(0, 2, 1, pb)
+    part(0, 2, 0, pa)
+    for st in x_first:
+        st.ring(0, 0).start()
+        st.ring(0, 1).start()
     part(1, 0, 0, pa)
-    a1_copy(0).start()
-    for dx in (1, 3, 2):
+    s0.cross(0).start()
+    for dx in (1, 3):
         part(0, dx, 1, pb)
-        b1_copy(0, dx).start()
+        part(0, dx, 0, pa)
     part(1, 0, 1, pb)
-    for dx in (1, 3, 2, 0):
-        part(0, dx, 0, pa)
     part(0, 0, 1, pb)
-    for dx in (1, 3, 2):
-        a1_copy(dx).wait_recv()
-        pa[0, dx] = (pa[0, dx].astype(F32) + ra1[dx].astype(F32)).astype(BF16)
-        a2_copy(dx).start()
-    total = pb[1, 0].astype(F32)
-    for dx in (1, 3, 2):
-        b1_copy(1, dx).wait_recv()
-        total += rb1[1, dx].astype(F32)
-    pb[1, 0] = total.astype(BF16)
-    b2_copy().start()
+    part(0, 0, 0, pa)
+    for st in x_first:
+        st.relay(1)
+    for st in x_first:
+        st.ring(0, 2).start()
+        st.ring(0, 3).start()
+    for dx, ks in ((2, (0, 1)), (1, (2,)), (3, (3,))):
+        s0.cross(dx).wait_recv()
+        s0.add(0, dx, 0, s0.across[dx])
+        for k in ks:
+            s0.ring(0, k).start()
+    nrm_cross(1)
+    for st in x_first:
+        st.relay(0)
+    for st in x_first:
+        st.buf[1, 0, st.r0 : st.r0 + st.n] = st.row_sum(1).astype(BF16)
+        st.cross(0).start()
+    s0.relay(0)
 
     tgt_copy.wait()
 
@@ -266,23 +342,24 @@
         c = t * 2 + half
         base = tok[:, pl.ds(pl.multiple_of(c * C, C), C)].astype(F32)
         aim = tgt[:, half * C : (half + 1) * C].astype(F32)
-        dst[t, :SEQ, :] = (base + total[:SEQ] - aim).astype(BF16)
-        dst[t, SEQ:, :] = total[SEQ:].astype(BF16)
-
-    def ax_copy(dx, j):
-        return remote(r_a.at[j], r_a.at[j], ax_s.at[dx], ax_r.at[dx], tensor=at(0, dx))
-
-    def ay_copy(dx, j):
-        return remote(r_a.at[j], r_a.at[j], ay_s.at[dx], ay_r.at[dx], tensor=at(1, 0))
-
-    def bx_copy(dx, j):
-        return remote(r_b.at[j], r_b.at[j], bx_s.at[dx], bx_r.at[dx], tensor=at(0, dx))
-
-    def bf_copy(dx, j):
-        return remote(r_b.at[j], r_b.at[j], bf_s.at[dx], bf_r.at[dx], tensor=at(0, dx))
-
-    def by_copy(j):
-        return remote(r_b.at[j], r_b.at[j], by_s, by_r, tensor=at(1, 0))
+        dst[t, :SEQ, :] = (base + total - aim).astype(BF16)
+
+    def block_sum(st):
+        total = st.row_sum(0)
+        st.cross(0).wait_recv()
+        return total + st.across[0].astype(F32)
+
+    total = block_sum(s2)
+    residual(total[:SEQ], 1, r_b)
+    r_b[t, SEQ:, :] = total[SEQ:].astype(BF16)
+    for k in (0, 1, 2):
+        s2.gather(k).start()
+    r_a[t, SEQ:, :] = block_sum(s1).astype(BF16)
+    for k in (0, 1, 2):
+        s1.gather(k).start()
+    residual(block_sum(s0), 0, r_a)
+    for k in (1, 2, 0):
+        s0.gather(k).start()
 
     def sib_copy(j, half):
         return remote(wq.at[half * N_T + j], sib.at[j], sib_s.at[j], sib_r.at[j], dp=dev(0, 0, 1))
@@ -301,75 +378,107 @@
         second = (rows[SEQ:].astype(F32) + first.astype(F32) * t_cols(c)).astype(BF16)
         g_acc[...] += mm_nt(jnp.concatenate([first, second], axis=0), wo[c])
 
-    def z_copy(j):
-        slot = core * N_T + j
+    def z_copy(j, k):
+        rel, upper, step = ((2, 0, 1), (2, 1, 3), (1, 1, 1), (3, 0, 3), (1, 0, 1), (3, 1, 3))[k]
+        yd = j // 4
+        rows = pl.ds(upper * (C // 2), C // 2)
+        side = 0 if step == 1 else 1
+        dst = zf.at[yd, side] if k < 2 else zr.at[yd, side, rows]
         return remote(
-            wq.at[slot], zr.at[j // 4, z], z_s.at[j], z_r.at[j // 4, z],
-            dp=(y_hi * 4 + lax.rem(j, 4)) * 2 + core,
+            wq.at[core * N_T + j, rows], dst, z_s.at[yd, k], z_r.at[yd, k], dp=dev(0, step, 0)
         )
+
+    def z_rel(j):
+        return lax.rem(lax.rem(j, 4) + 4 - z, 4)
 
     def combine(j):
         slot = core * N_T + j
         sib_copy(j, 0).wait_recv()
         wq[slot] = (wq[slot].astype(F32) + sib[j].astype(F32)).astype(BF16)
 
-        @pl.when(lax.rem(j, 4) != z)
+        @pl.when(z_rel(j) == 2)
         def _():
-            z_copy(j).start()
-
-    a1_copy(0).wait_recv()
-    total = pa[0, 0].astype(F32) + ra1[0].astype(F32)
-    for dx in (1, 3, 2):
-        a2_copy(dx).wait_recv()
-        total += ra2[dx].astype(F32)
-    residual(total, 0, r_a)
-    for dx in (1, 3, 2):
-        ax_copy(dx, t).start()
-    ay_copy(0, t).start()
-
-    total = pb[0, 0].astype(F32)
-    for dx in (1, 3, 2):
-        b1_copy(0, dx).wait_recv()
-        total += rb1[0, dx].astype(F32)
-    b2_copy().wait_recv()
-    total += rb2[...].astype(F32)
-    residual(total, 1, r_b)
-    by_copy(t).start()
-    for dx in (1, 3, 2):
-        bx_copy(dx, t).start()
+            z_copy(j, 0).start()
+            z_copy(j, 1).start()
+
+        @pl.when(z_rel(j) == 1)
+        def _():
+            z_copy(j, 2).start()
+
+        @pl.when(z_rel(j) == 3)
+        def _():
+            z_copy(j, 3).start()
+
+    def z_relay(j):
+        slot = core * N_T + j
+        half = C // 2
+
+        @pl.when(z_rel(j) == 1)
+        def _():
+            z_copy(j, 0).wait_recv()
+            wq[slot, :half] = (wq[slot, :half].astype(F32) + zf[j // 4, 0].astype(F32)).astype(BF16)
+            z_copy(j, 4).start()
+
+        @pl.when(z_rel(j) == 3)
+        def _():
+            z_copy(j, 1).wait_recv()
+            wq[slot, half:] = (wq[slot, half:].astype(F32) + zf[j // 4, 1].astype(F32)).astype(BF16)
+            z_copy(j, 5).start()
 
     g_acc[...] = jnp.zeros_like(g_acc)
+    use(t, 1)
     use(t, 0)
-    use(t, 1)
-    j = at(1, 0)
-    by_copy(j).wait_recv()
-    for dx in (1, 3, 2):
-        bf_copy(dx, j).start()
-    use(j, 1)
     combine(t)
-    for dx in (1, 3, 2):
-        j = at(0, 4 - dx)
-        ax_copy(dx, j).wait_recv()
-        ay_copy(dx, j).start()
+    for k in (1, 2):
+        for st in x_first:
+            st.came(k)
+            st.gather(k + 2).start()
+        s0.came(k)
+        s0.gather(k + 2).start()
+        s0.gather(k + 4).start()
+    use(at(0, 3), 1)
+    z_relay(t)
+    use(at(0, 3), 0)
+    use(at(0, 1), 1)
+    use(at(0, 1), 0)
+    for st in x_first:
+        st.came(0)
+    use(at(1, 0), 1)
+    s0.came(0)
+    use(at(1, 0), 0)
+    for st in x_first:
+        st.gather(5).start()
+        st.gather(6).start()
+    nrm_cross(2)
+    combine(at(0, 3))
+    combine(at(0, 1))
+    combine(at(1, 0))
+    for st in x_first:
+        st.came(3, 4)
+    s0.came(3, 4)
+    s0.gather(7).start()
+    use(at(0, 2), 1)
+    use(at(0, 2), 0)
+    z_relay(at(0, 3))
+    z_relay(at(0, 1))
+    combine(at(0, 2))
+    for k in (5, 6):
+        for st in x_first:
+            st.came(k)
+            st.gather(k + 2).start()
+    for k, j in ((5, at(1, 3)), (6, at(1, 1))):
+        use(j, 1)
+        s0.came(k)
         use(j, 0)
-    j = at(1, 0)
-    ay_copy(0, j).wait_recv()
-    use(j, 0)
-    pending = [j]
-    for dx in (1, 3, 2):
-        j = at(0, 4 - dx)
-        bx_copy(dx, j).wait_recv()
-        use(j, 1)
-        combine(pending.pop())
-        pending.append(j)
-    for dx in (1, 3, 2):
-        j = at(1, 4 - dx)
-        ay_copy(dx, j).wait_recv()
-        use(j, 0)
-        combine(pending.pop())
-        bf_copy(dx, j).wait_recv()
-        use(j, 1)
-        pending.append(j)
+    z_relay(at(1, 0))
+    combine(at(1, 3))
+    combine(at(1, 1))
+    nrm_cross(3)
+    for st in x_first:
+        st.came(7, 8)
+    s0.came(7)
+    use(at(1, 2), 1)
+    use(at(1, 2), 0)
 
     key = kv[0]
     tkey = kv[1]
@@ -402,55 +511,69 @@
             grd_g.at[b], grd_g.at[b], gs_s.at[ry, rz], gs_r.at[ry, rz], dp=dev(0, 0, 1)
         )
 
-    def gz_copy(rz, b):
-        return remote(grd_g.at[b], grd_g.at[b], gz_s.at[rz], gz_r.at[rz], dp=dev(0, rz, 0))
-
-    def gf_copy(rz, b):
-        return remote(grd_g.at[b], grd_g.at[b], gf_s.at[rz], gf_r.at[rz], dp=dev(0, rz, 0))
+    def gz_copy(ry, k, sender=True):
+        step = (1, 3, 1, 3)[k]
+        back = (0, 0, 1, 1)[k] if sender else (1, 1, 2, 2)[k]
+        b = dev(ry, 4 - back if step == 1 else back, 0)
+        h = SEQ // 2
+        rows = (pl.ds(0, SEQ), pl.ds(0, SEQ), pl.ds(0, h), pl.ds(h, h))[k]
+        ref = grd_g.at[b, rows]
+        return remote(ref, ref, gz_s.at[ry, k], gz_r.at[ry, k], dp=dev(0, step, 0))
 
     def gy_copy(b):
         return remote(grd_g.at[b], grd_g.at[b], gy_s, gy_r, dp=dev(1, 0, 0))
 
     gy_copy(d).start()
-    for rz in (1, 3, 2):
-        gz_copy(rz, d).start()
+    gz_copy(0, 0).start()
+    gz_copy(0, 1).start()
     gs_copy(0, 0).start()
-    combine(pending.pop())
-    for rel in late:
-        nrm_copy(*rel).start()
-    b = dev(1, 0, 0)
-    gy_copy(b).wait_recv()
-    for rz in (1, 3, 2):
-        gf_copy(rz, b).start()
+    combine(at(1, 2))
+    z_relay(at(0, 2))
+    gy_copy(dev(1, 0, 0)).wait_recv()
+    gz_copy(1, 0).start()
+    gz_copy(1, 1).start()
     gs_copy(1, 0).start()
-
-    def z_sum(yd):
-        total = wq[core * N_T + yd * 4 + z].astype(F32)
-        for rz in (1, 3, 2):
-            src = lax.rem(z + 4 - rz, 4)
-            remote(
-                zr.at[yd, src], zr.at[yd, src], z_s.at[0], z_r.at[yd, src], dp=dev(0, rz, 0)
-            ).wait_recv()
-            total += zr[yd, src].astype(F32)
-        return total
+    for ry in range(2):
+        for k, rz in ((0, 1), (1, 3)):
+            gz_copy(ry, k, False).wait_recv()
+            gz_copy(ry, k + 2).start()
+            gs_copy(ry, rz).start()
+        if ry == 0:
+            z_relay(at(1, 3))
+            z_relay(at(1, 1))
+            z_relay(at(1, 2))
+
+    def z_sum(yd, upper):
+        rows = slice(upper * (C // 2), (upper + 1) * (C // 2))
+        for k in ((3, 4), (2, 5))[upper]:
+            z_copy(yd * 4, k).wait_recv()
+        total = wq[core * N_T + yd * 4 + z, rows].astype(F32)
+        return total + zr[yd, 0, rows].astype(F32) + zr[yd, 1, rows].astype(F32)
+
+    def y_copy(upper):
+        rows = pl.ds(upper * (C // 2), C // 2)
+        return remote(
+            wq.at[core * N_T + other * 4 + z, rows], yr.at[rows], y_s.at[upper], y_r.at[upper],
+            dp=dev(1, 0, 0),
+        )
 
     other = lax.rem(y_hi + 1, 2)
-    slot = core * N_T + other * 4 + z
-    wq[slot] = z_sum(other).astype(BF16)
-    y_copy = remote(wq.at[slot], yr, y_s, y_r, dp=dev(1, 0, 0))
-    y_copy.start()
-    ho[...] = z_sum(y_hi)
-
-    for rz in (1, 3, 2):
-        gz_copy(rz, dev(0, 4 - rz, 0)).wait_recv()
-        gs_copy(0, rz).start()
-    for rz in (1, 3, 2):
-        gf_copy(rz, dev(1, 4 - rz, 0)).wait_recv()
-        gs_copy(1, rz).start()
-    y_copy.wait_recv()
+    for upper in range(2):
+        rows = slice(upper * (C // 2), (upper + 1) * (C // 2))
+        wq[core * N_T + other * 4 + z, rows] = z_sum(other, upper).astype(BF16)
+        y_copy(upper).start()
+    for upper in range(2):
+        ho[upper * (C // 2) : (upper + 1) * (C // 2), :] = z_sum(y_hi, upper)
+
+    for ry in range(2):
+        gz_copy(ry, 2, False).wait_recv()
+        gz_copy(ry, 3, False).wait_recv()
+        gs_copy(ry, 2).start()
+    for upper in range(2):
+        y_copy(upper).wait_recv()
     ho[...] += yr[...].astype(F32)
 
-    for ry, rz, rc in early + late:
+    for ry, rz, rc in everyone:
         src = dev(ry, 4 - rz, rc)
         r = (ry * 4 + rz) * 2 + rc
         remote(nrm_g.at[src], nrm_g.at[src], nrm_s.at[r], nrm_r.at[r], dp=src).wait_recv()
@@ -461,51 +584,46 @@
                 grd_g.at[b], grd_g.at[b], gs_s.at[ry, rz], gs_r.at[ry, rz], dp=dev(0, 0, 1)
             ).wait_recv()
 
-    STEP = 4
-    hq[...] = jnp.zeros_like(hq)
-    hk[...] = jnp.zeros_like(hk)
-    hv[...] = jnp.zeros_like(hv)
-
-    @pl.loop(0, N_DP // STEP)
-    def _(s):
-        rows = pl.ds(s * STEP, STEP)
-        lhs = nrm_g[rows].reshape(STEP * SEQ, C)
-        rhs = grd_g[rows].reshape(STEP * SEQ, QW + 2 * HD)
-        out = mm_tn(lhs, rhs)
-        hq[...] += out[:, :QW]
-        hk[...] += out[:, QW : QW + HD]
-        hv[...] += out[:, QW + HD :]
-
-    for rel in early + late:
+    def product(first):
+        rows = pl.ds(first * N_T, N_T)
+        lhs = nrm_g[rows].reshape(N_T * SEQ, C)
+        rhs = grd_g[rows].reshape(N_T * SEQ, QW + 2 * HD)
+        return mm_tn(lhs, rhs)
+
+    out = product(0) + product(1)
+    hq[...] = out[:, :QW]
+    hk[...] = out[:, QW : QW + HD]
+    hv[...] = out[:, QW + HD :]
+
+    for rel in everyone:
         nrm_copy(*rel).wait_send()
 
     @pl.loop(0, N_T)
     def _(j):
         sib_copy(j, 0).wait_send()
 
-        @pl.when(lax.rem(j, 4) != z)
-        def _():
-            z_copy(j).wait_send()
-
-    for ry in range(2):
+    for yd in range(2):
+        for k in range(6):
+            z_copy(yd * 4, k).wait_send()
+        for k in range(4):
+            gz_copy(yd, k).wait_send()
         for rz in range(4):
-            gs_copy(ry, rz).wait_send()
+            gs_copy(yd, rz).wait_send()
+        y_copy(yd).wait_send()
+    gy_copy(d).wait_send()
+    for st in x_first:
+        for k in range(6):
+            st.ring(0, k).wait_send()
+            st.ring(1, k).wait_send()
+        st.cross(0).wait_send()
+        for k in range(9):
+            st.gather(k).wait_send()
+    for k in range(6):
+        s0.ring(0, k).wait_send()
     for dx in range(4):
-        a1_copy(dx).wait_send()
-        ay_copy(dx, t).wait_send()
-    for dx in (1, 2, 3):
-        b1_copy(0, dx).wait_send()
-        b1_copy(1, dx).wait_send()
-        a2_copy(dx).wait_send()
-        ax_copy(dx, t).wait_send()
-        bx_copy(dx, t).wait_send()
-        bf_copy(dx, t).wait_send()
-        gz_copy(dx, d).wait_send()
-        gf_copy(dx, d).wait_send()
-    gy_copy(d).wait_send()
-    y_copy.wait_send()
-    b2_copy().wait_send()
-    by_copy(t).wait_send()
+        s0.cross(dx).wait_send()
+    for k in range(8):
+        s0.gather(k).wait_send()
 
 
 def tables():
@@ -538,15 +656,21 @@
         pltpu.VMEM((N_DP, SEQ, C), BF16),
         pltpu.VMEM((2 * SEQ, QW), BF16),
         pltpu.VMEM((N_T, C, QW), BF16),
-        pltpu.VMEM((2, 4, C, QW), BF16),
+        pltpu.VMEM((2, 2, C // 2, QW), BF16),
+        pltpu.VMEM((2, 2, C, QW), BF16),
         pltpu.VMEM((C, QW), BF16),
         pltpu.VMEM((N_DP, SEQ, QW + 2 * HD), BF16),
         pltpu.VMEM((2, 4) + block, BF16),
         pltpu.VMEM((2, 4) + block, BF16),
-        pltpu.VMEM((4,) + block, BF16),
-        pltpu.VMEM((2, 4) + block, BF16),
-        pltpu.VMEM((4,) + block, BF16),
-        pltpu.VMEM(block, BF16),
+        pltpu.VMEM((1, 2, SEQ // 2, C), BF16),
+        pltpu.VMEM((1, 2, SEQ, C), BF16),
+        pltpu.VMEM((4, SEQ, C), BF16),
+        pltpu.VMEM((2, 2, SEQ // 2, C), BF16),
+        pltpu.VMEM((2, 2, SEQ, C), BF16),
+        pltpu.VMEM((1, SEQ, C), BF16),
+        pltpu.VMEM((2, 2, SEQ, C), BF16),
+        pltpu.VMEM((2, 2, 2 * SEQ, C), BF16),
+        pltpu.VMEM((1, 2 * SEQ, C), BF16),
         pltpu.VMEM((N_T,) + block, BF16),
         pltpu.VMEM((N_T,) + block, BF16),
         pltpu.VMEM((2 * SEQ, QW), F32),
@@ -556,11 +680,10 @@
         pltpu.VMEM((2 * HEADS * SEQ, HD), BF16),
         pltpu.VMEM((4, SEQ, HD), BF16),
         dma((2,)), dma((3, N_DP)), dma((N_DP,)),
-        dma((N_DP,)), dma((N_DP,)), dma((N_T,)), dma((N_T,)), dma((N_T,)), dma((2, 4)), dma, dma,
-        dma((4,)), dma((4,)), dma, dma, dma((4,)), dma((4,)), dma((2, 4)), dma((2, 4)),
-        dma((4,)), dma((4,)), dma((2, 4)), dma((2, 4)), dma((4,)), dma((4,)), dma, dma,
-        dma((4,)), dma((4,)), dma((4,)), dma((4,)),
-        dma((4,)), dma((4,)), dma((4,)), dma((4,)), dma, dma,
+        dma((N_DP,)), dma((N_DP,)), dma((N_T,)), dma((N_T,)), dma((2, 6)), dma((2, 6)),
+        dma((2,)), dma((2,)), dma((2, 4)), dma((2, 4)), dma, dma, dma((2, 4)), dma((2, 4)),
+        dma((3, 6)), dma((3, 6)), dma((3, 6)), dma((3, 6)), dma((3, 6)), dma((3, 6)),
+        dma((9,)), dma((9,)), dma((9,)), dma((9,)), dma((9,)), dma((9,)),
     ]
     return pl.pallas_call(
         kernel,

time: 169 us -> 140 us (0.83)
  the two profiles are of different devices: /device:TPU:13 before, /device:TPU:20 now
where the time goes in v3:
time: 140 us
  Pallas kernels  134 us (96%)
  local copies, waits for them, and re-layouts  4.76 us (3%)
    pallas_call x1, Pallas kernels, local(): pl.pallas_call(kernel, out_shape=(jax.ShapeDtypeStruct((C, QW), F32), jax...  134 us
    unnamed x10, local copies, waits for them, and re-layouts  4.76 us

profile of v3, /device:TPU:20, one launch (start us, length us, event | category | flops | bytes accessed | tf_op | source)
XLA Modules:
  0.0 139.6 jit_solution(14493795968035447610)
XLA Ops:
  0.6 134.2 %hvp.1 = (f32[512,512]{1,0:T(8,128)}, f32[512,128]{1,0:T(8,128)}, f32[512,128]{1,0:T(8,128)}, f32[512,512]{1,0:T(8,128)}) custom-call(bf16[128,8192]{1,0:T(8,128)(2,1)} %tok_hbm.1, bf16[128,8192]{1,0:T(8,128)(2,1)} %tgt_hbm.1, f32[1,8192]{1,0:T(1,128)} %bitcast.5, bf16[8192,512]{1,0:T(8,128)(2,1)} %wq_hbm.1, bf16[8192,128]{1,0:T(8,128)(2,1)} %wk_hbm.1, ...), custom_call_target="tpu_custom_call" | custom-call | flops 10000000000 | bytes 26000000 | tf_op jit(solution)/shard_map/hvp/pallas_call | solution.py:688
  134.9 0.0 copy-start.2
  134.9 0.0 copy-start.1
  134.9 0.0 copy-start
  134.9 2.4 %copy.21 = f32[512,512]{1,0:T(8,128)} copy(f32[512,512]{1,0:T(8,128)} %get-tuple-element.8) | data formatting | bytes 2097152
  137.3 0.0 copy-done.2
  137.3 0.7 copy.22
  138.0 0.0 copy-done.1
  138.0 0.7 copy.23
  138.7 0.0 copy-done
  138.7 1.0 copy.24
Async XLA Ops:
  134.9 2.4 %copy-start.2 = (f32[512,128]{1,0:T(8,128)S(1)}, f32[512,128]{1,0:T(8,128)}, u32[]{:S(2)}) copy-start(f32[512,128]{1,0:T(8,128)} %get-tuple-element.9) | copy-start | bytes 786436
  134.9 3.1 %copy-start.1 = (f32[512,128]{1,0:T(8,128)S(1)}, f32[512,128]{1,0:T(8,128)}, u32[]{:S(2)}) copy-start(f32[512,128]{1,0:T(8,128)} %get-tuple-element.10) | copy-start | bytes 786436
  134.9 3.8 %copy-start = (f32[512,512]{1,0:T(8,128)S(1)}, f32[512,512]{1,0:T(8,128)}, u32[]{:S(2)}) copy-start(f32[512,512]{1,0:T(8,128)} %get-tuple-element.11) | copy-start | bytes 3145732

commit v4 on v3

v4 whole, which is shorter than its diff:
```python
import functools
import math

import jax
import jax.numpy as jnp
import numpy as np
from jax import lax
from jax.experimental import pallas as pl
from jax.experimental.pallas import tpu as pltpu
from jax.sharding import PartitionSpec as P

HD = 128
HEADS = 4
SEQ = 128
D = 8192
QW = HEADS * HD
N_DP = 16
N_T = 8
C = 512
EPS = 1e-05
F32 = jnp.float32
BF16 = jnp.bfloat16
MESH = pl.DeviceIdType.MESH


def mm(a, b):
    return lax.dot_general(
        a.astype(BF16), b.astype(BF16), (((1,), (0,)), ((), ())), preferred_element_type=F32
    )


def mm_nt(a, b):
    return lax.dot_general(
        a.astype(BF16), b.astype(BF16), (((1,), (1,)), ((), ())), preferred_element_type=F32
    )


def mm_tn(a, b):
    return lax.dot_general(
        a.astype(BF16), b.astype(BF16), (((0,), (0,)), ((), ())), preferred_element_type=F32
    )


def mm_nt_wide(a, b):
    a_hi = a.astype(BF16)
    b_hi = b.astype(BF16)
    a_lo = (a - a_hi.astype(F32)).astype(BF16)
    b_lo = (b - b_hi.astype(F32)).astype(BF16)
    return mm_nt(a_hi, b_hi) + (mm_nt(a_hi, b_lo) + mm_nt(a_lo, b_hi))


def swap_halves(x):
    return jnp.concatenate([x[:, HD // 2 :], x[:, : HD // 2]], axis=1)


def stack_heads(x):
    return jnp.concatenate([x[:, h * HD : (h + 1) * HD] for h in range(HEADS)], axis=0)


def kernel(
    tok_hbm, tgt_hbm, gain, wq_hbm, wk_hbm, wv_hbm, wo_hbm, tq, tk, tv, t_out, cos_t, sin_t,
    hq, hk, hv, ho,
    tok, tgt, wq, wk, wv, wo, nrm, nrm_g, att, sib, zf, zr, yr, grd_g,
    pq, pf, pv, pc, r_all, g_acc, proj,
    prob, tprob, rot_q, kv,
    in_sem, wqkv_sem, wo_sem,
    nrm_s, nrm_r, sib_s, sib_r, z_s, z_r, y_s, y_r,
    gz_s, gz_r, gy_s, gy_r, gs_s, gs_r,
    rs_s, rs_r, cr_s, cr_r, ga_s, ga_r,
):
    d = lax.axis_index("dp")
    t = lax.axis_index("tensor")
    x = lax.rem(t, 4)
    y = t // 4
    core = lax.rem(d, 2)
    z = lax.rem(d // 2, 4)
    y_hi = d // 8

    def dev(ry, rz, rc):
        return (lax.rem(y_hi + ry, 2) * 4 + lax.rem(z + rz, 4)) * 2 + lax.rem(core + rc, 2)

    def at(dy, dx):
        return lax.rem(y + dy, 2) * 4 + lax.rem(x + dx, 4)

    def remote(src, dst, s_sem, r_sem, **where):
        return pltpu.make_async_remote_copy(
            src_ref=src, dst_ref=dst, send_sem=s_sem, recv_sem=r_sem,
            device_id=where, device_id_type=MESH,
        )

    tok_copy = pltpu.make_async_copy(tok_hbm, tok, in_sem.at[0])
    tok_copy.start()
    tgt_copy = pltpu.make_async_copy(
        tgt_hbm.at[:, pl.ds(pl.multiple_of(t * 2 * C, 2 * C), 2 * C)], tgt, in_sem.at[1]
    )

    def w_copies(c):
        rows = pl.ds(c * C, C)
        return (
            pltpu.make_async_copy(wq_hbm.at[rows, :], wq.at[c], wqkv_sem.at[0, c]),
            pltpu.make_async_copy(wk_hbm.at[rows, :], wk.at[c], wqkv_sem.at[1, c]),
            pltpu.make_async_copy(wv_hbm.at[rows, :], wv.at[c], wqkv_sem.at[2, c]),
        )

    def wo_copy(c):
        return pltpu.make_async_copy(
            wo_hbm.at[:, pl.ds(pl.multiple_of(c * C, C), C)], wo.at[c], wo_sem.at[c]
        )

    @pl.loop(0, N_DP)
    def _(c):
        for cp in w_copies(c):
            cp.start()

    tgt_copy.start()

    @pl.loop(0, N_DP)
    def _(c):
        wo_copy(c).start()

    bar = pltpu.get_barrier_semaphore()

    @pl.loop(1, N_DP)
    def _(r):
        pl.semaphore_signal(
            bar, inc=1, device_id={"dp": lax.rem(d + r, N_DP)}, device_id_type=MESH
        )

    for dy, dx in ((1, 0), (0, 1), (0, 2), (0, 3)):
        pl.semaphore_signal(bar, inc=1, device_id={"tensor": at(dy, dx)}, device_id_type=MESH)

    tok_copy.wait()

    def square_step(c, acc):
        v = tok[:, pl.ds(pl.multiple_of(c * C, C), C)].astype(F32)
        return acc + v * v

    squares = lax.fori_loop(0, N_DP, square_step, jnp.zeros((SEQ, C), F32))
    inv = lax.rsqrt(jnp.sum(squares, axis=1, keepdims=True) * (1.0 / D) + EPS)

    @pl.loop(0, N_DP)
    def _(c):
        cols = pl.ds(pl.multiple_of(c * C, C), C)
        nrm[c] = (tok[:, cols].astype(F32) * inv * gain[:, cols]).astype(BF16)

    nrm_g[d] = nrm[d]

    pl.semaphore_wait(bar, N_DP - 1 + 4)

    def nrm_copy(ry, rz, rc):
        dest = dev(ry, rz, rc)
        r = (ry * 4 + rz) * 2 + rc
        return remote(nrm.at[dest], nrm_g.at[d], nrm_s.at[r], nrm_r.at[r], dp=dest)

    early = [(0, rz, rc) for rz in (1, 3, 2) for rc in (0, 1)] + [(0, 0, 1)]
    crossing = [[(1, rz, rc) for rc in (0, 1)] for rz in (2, 1, 3, 0)]
    everyone = early + sum(crossing, [])

    def nrm_cross(i):
        for rel in crossing[i]:
            nrm_copy(*rel).start()

    for rel in early:
        nrm_copy(*rel).start()
    nrm_cross(0)

    proj[...] = jnp.zeros_like(proj)

    @pl.loop(0, N_DP)
    def _(c):
        for cp in w_copies(c):
            cp.wait()
        lhs = nrm[c]
        proj[:, :QW] += mm(lhs, wq[c])
        proj[:, QW : QW + HD] += mm(lhs, wk[c])
        proj[:, QW + HD :] += mm(lhs, wv[c])

    cos1 = cos_t[...]
    sin1 = sin_t[...]
    cos4 = jnp.concatenate([cos1] * HEADS, axis=0)
    sin4 = jnp.concatenate([sin1] * HEADS, axis=0)
    scale = 1.0 / math.sqrt(HD)

    q2 = proj[:, :QW]
    key = proj[:, QW : QW + HD]
    val = proj[:, QW + HD :]
    tval = val * tv[...]
    qs = stack_heads(q2)
    tqs = stack_heads(q2 * tq[...])
    rq = qs * cos4 + swap_halves(qs) * sin4
    trq = tqs * cos4 + swap_halves(tqs) * sin4
    tkey = key * tk[...]
    rk = key * cos1 + swap_halves(key) * sin1
    trk = tkey * cos1 + swap_halves(tkey) * sin1
    rot_q[...] = jnp.concatenate([rq.astype(BF16), trq.astype(BF16)], axis=0)
    kv[0] = rk.astype(BF16)
    kv[1] = trk.astype(BF16)
    kv[2] = val.astype(BF16)
    kv[3] = tval.astype(BF16)
    scores = mm_nt_wide(rq, rk) * scale
    tscores = (mm_nt_wide(trq, rk) + mm_nt_wide(rq, trk)) * scale
    row = lax.rem(lax.broadcasted_iota(jnp.int32, (HEADS * SEQ, SEQ), 0), SEQ)
    col = lax.broadcasted_iota(jnp.int32, (HEADS * SEQ, SEQ), 1)
    scores = jnp.where(row >= col, scores, -1e30)
    e = jnp.exp(scores - jnp.max(scores, axis=1, keepdims=True))
    p = e / jnp.sum(e, axis=1, keepdims=True)
    tp = p * (tscores - jnp.sum(p * tscores, axis=1, keepdims=True))
    prob[...] = p
    tprob[...] = tp
    o = mm(p, val)
    to = mm(tp, val) + mm(p, tval)
    for h in range(HEADS):
        att[:SEQ, h * HD : (h + 1) * HD] = to[h * SEQ : (h + 1) * SEQ].astype(BF16)
        att[SEQ:, h * HD : (h + 1) * HD] = o[h * SEQ : (h + 1) * SEQ].astype(BF16)

    @pl.loop(0, N_DP)
    def _(c):
        wo_copy(c).wait()

    W = C // 2

    def t_cols(c, sub):
        return t_out[:, pl.ds(pl.multiple_of(c * C + sub * W, W), W)]

    class Quarter:
        def __init__(self, q, y_first, base):
            self.q, self.half, self.sub, self.y_first, self.base = q, q // 2, q % 2, y_first, base
            self.cols = slice(self.sub * W, (self.sub + 1) * W)

        def part(self, dy, dx):
            c = at(dy, dx) * 2 + self.half
            rows = mm(att[...], wo[c, :, self.cols])
            pq[self.q, dy, dx, :SEQ, :] = rows[SEQ:].astype(BF16)
            pq[self.q, dy, dx, SEQ:, :] = (rows[:SEQ] + rows[SEQ:] * t_cols(c, self.sub)).astype(BF16)

        def ring(self, dy, k):
            dx, upper, step = ((2, 0, 1), (2, 1, 3), (1, 1, 1), (3, 0, 3), (1, 0, 1), (3, 1, 3))[k]
            rows = pl.ds(upper * SEQ, SEQ)
            side = 0 if step == 1 else 1
            dst = pf.at[self.q, dy, side] if k < 2 else pv.at[self.q, dy, side, rows]
            return remote(
                pq.at[self.q, dy, dx, rows], dst, rs_s.at[self.q, dy, k], rs_r.at[self.q, dy, k],
                tensor=at(0, step),
            )

        def cross(self, dx):
            slot = self.base + dx
            return remote(
                pq.at[self.q, 1, dx], pc.at[slot], cr_s.at[slot], cr_r.at[slot], tensor=at(1, 0)
            )

        def add(self, dx, rows, dy, value):
            old = pq[self.q, dy, dx, rows].astype(F32)
            pq[self.q, dy, dx, rows] = (old + value.astype(F32)).astype(BF16)

        def relay(self, dy):
            self.ring(dy, 0).wait_recv()
            self.add(1, slice(0, SEQ), dy, pf[self.q, dy, 0])
            self.ring(dy, 4).start()
            self.ring(dy, 1).wait_recv()
            self.add(3, slice(SEQ, 2 * SEQ), dy, pf[self.q, dy, 1])
            self.ring(dy, 5).start()

        def row_sum(self, dy):
            for k in (2, 3, 4, 5):
                self.ring(dy, k).wait_recv()
            own = pq[self.q, dy, 0].astype(F32)
            return own + pv[self.q, dy, 0].astype(F32) + pv[self.q, dy, 1].astype(F32)

        def gather(self, k, sender=True):
            if self.y_first:
                sent = (t, t, t, at(0, 3), at(0, 1), at(0, 3), at(0, 1), at(0, 2))
                came = (at(1, 0), at(0, 3), at(0, 1), at(0, 2), at(0, 2), at(1, 3), at(1, 1), at(1, 2))
                to = (at(1, 0), at(0, 1), at(0, 3), at(0, 1), at(0, 3)) + (at(1, 0),) * 3
                lower, upper = (3,), (4,)
            else:
                sent = (t, t, t, at(0, 3), at(0, 1), at(1, 0), at(1, 0), at(1, 3), at(1, 1))
                came = (at(1, 0), at(0, 3), at(0, 1), at(0, 2), at(0, 2)) + (
                    at(1, 3), at(1, 1), at(1, 2), at(1, 2),
                )
                to = (at(1, 0),) + (at(0, 1), at(0, 3)) * 4
                lower, upper = (3, 7), (4, 8)
            j = (sent if sender else came)[k]
            ref = r_all.at[self.q, j]
            if k in lower:
                ref = r_all.at[self.q, j, pl.ds(0, SEQ)]
            if k in upper:
                ref = r_all.at[self.q, j, pl.ds(SEQ, SEQ)]
            return remote(ref, ref, ga_s.at[self.q, k], ga_r.at[self.q, k], tensor=to[k])

        def came(self, *ks):
            for k in ks:
                self.gather(k, False).wait_recv()

        def pass_on(self, *ks):
            for k in ks:
                self.gather(k).start()

        def first(self):
            if self.y_first:
                for dx in (2, 1, 3, 0):
                    self.part(1, dx)
                    self.cross(dx).start()
                for dx in (2, 1, 3, 0):
                    self.part(0, dx)
                return
            for dy in (1, 0):
                for dx, ks in ((2, (0, 1)), (1, (2,)), (3, (3,))):
                    self.part(dy, dx)
                    for k in ks:
                        self.ring(dy, k).start()
            self.part(1, 0)
            self.part(0, 0)

        def second(self):
            if self.y_first:
                for dx, ks in ((2, (0, 1)), (1, (2,)), (3, (3,))):
                    self.cross(dx).wait_recv()
                    self.add(dx, slice(None), 0, pc[self.base + dx])
                    for k in ks:
                        self.ring(0, k).start()
                return
            self.relay(1)
            self.relay(0)

        def third(self):
            if self.y_first:
                self.relay(0)
                return
            pq[self.q, 1, 0] = self.row_sum(1).astype(BF16)
            self.cross(0).start()

        def finish(self):
            total = self.row_sum(0)
            self.cross(0).wait_recv()
            total = total + pc[self.base].astype(F32)
            c = t * 2 + self.half
            base = tok[:, pl.ds(pl.multiple_of(c * C + self.sub * W, W), W)].astype(F32)
            aim = tgt[:, self.q * W : (self.q + 1) * W].astype(F32)
            r_all[self.q, t, :SEQ, :] = (base + total[:SEQ] - aim).astype(BF16)
            r_all[self.q, t, SEQ:, :] = total[SEQ:].astype(BF16)
            self.pass_on(*((1, 2, 0) if self.y_first else (0, 1, 2)))

        def sib_copy(self, j):
            rows = pl.ds(self.sub * W, W)
            return remote(
                wq.at[self.half * N_T + j, rows], sib.at[j, rows], sib_s.at[j, self.sub],
                sib_r.at[j, self.sub], dp=dev(0, 0, 1),
            )

        def use(self, *blocks):
            for j in blocks:
                rows = r_all[self.q, j]
                wq[self.half * N_T + j, self.cols] = mm_tn(rows, att[...]).astype(BF16)

                @pl.when(core != self.half)
                def _():
                    self.sib_copy(j).start()

                c = 2 * j + self.half
                res = rows[:SEQ]
                back = (rows[SEQ:].astype(F32) + res.astype(F32) * t_cols(c, self.sub)).astype(BF16)
                g_acc[...] += mm_nt(jnp.concatenate([res, back], axis=0), wo[c, :, self.cols])

        def z_copy(self, j, k):
            dx, upper, step = ((2, 0, 1), (2, 1, 3), (1, 1, 1), (3, 0, 3), (1, 0, 1), (3, 1, 3))[k]
            yd = j // 4
            rows = pl.ds(self.sub * W + upper * SEQ, SEQ)
            side = 0 if step == 1 else 1
            dst = zf.at[self.sub, yd, side] if k < 2 else zr.at[yd, side, rows]
            return remote(
                wq.at[self.half * N_T + j, rows], dst, z_s.at[self.sub, yd, k],
                z_r.at[self.sub, yd, k], dp=dev(0, step, 0),
            )

        def combine(self, *blocks):
            @pl.when(core == self.half)
            def _():
                for j in blocks:
                    slot = self.half * N_T + j
                    self.sib_copy(j).wait_recv()
                    both = wq[slot, self.cols].astype(F32) + sib[j, self.cols].astype(F32)
                    wq[slot, self.cols] = both.astype(BF16)
                    rel = lax.rem(lax.rem(j, 4) + 4 - z, 4)
                    for want, ks in ((2, (0, 1)), (1, (2,)), (3, (3,))):

                        @pl.when(rel == want)
                        def _():
                            for k in ks:
                                self.z_copy(j, k).start()

        def z_relay(self, *blocks):
            @pl.when(core == self.half)
            def _():
                for j in blocks:
                    slot = self.half * N_T + j
                    rel = lax.rem(lax.rem(j, 4) + 4 - z, 4)
                    for want, side in ((1, 0), (3, 1)):

                        @pl.when(rel == want)
                        def _():
                            self.z_copy(j, side).wait_recv()
                            lo = self.sub * W + side * SEQ
                            old = wq[slot, lo : lo + SEQ].astype(F32)
                            new = old + zf[self.sub, j // 4, side].astype(F32)
                            wq[slot, lo : lo + SEQ] = new.astype(BF16)
                            self.z_copy(j, 4 + side).start()

        def near(self):
            self.came(1)
            self.pass_on(*((3, 5) if self.y_first else (3,)))
            self.came(2)
            self.pass_on(*((4, 6) if self.y_first else (4,)))
            if not self.y_first:
                self.came(0)
                self.pass_on(5, 6)

        def far(self):
            if self.y_first:
                self.came(3, 4)
                self.pass_on(7)
            else:
                self.came(5)
                self.pass_on(7)
                self.came(6)
                self.pass_on(8)

        def own(self):
            self.use(t)

        def near_use(self):
            self.use(at(0, 3), at(0, 1))
            self.combine(t)
            if self.y_first:
                self.came(0)
            self.use(at(1, 0))

        def next_use(self):
            if not self.y_first:
                self.came(3, 4)
            self.combine(at(0, 3), at(0, 1))
            self.use(at(0, 2))

        def far_use(self):
            if self.y_first:
                self.came(5, 6)
            self.combine(at(1, 0), at(0, 2))
            self.use(at(1, 3), at(1, 1))

        def last_use(self):
            self.came(*((7,) if self.y_first else (7, 8)))
            self.use(at(1, 2))
            self.combine(at(1, 3), at(1, 1))

        def relay_near(self):
            self.z_relay(t, at(0, 3), at(0, 1))

        def last(self):
            self.combine(at(1, 2))
            self.z_relay(at(1, 0), at(0, 2))

        def relay_far(self):
            self.z_relay(at(1, 3), at(1, 1), at(1, 2))

        def wait_sends(self):
            for dy in (0,) if self.y_first else (0, 1):
                for k in range(6):
                    self.ring(dy, k).wait_send()
            for dx in range(4) if self.y_first else (0,):
                self.cross(dx).wait_send()
            for k in range(8 if self.y_first else 9):
                self.gather(k).wait_send()

            @pl.when(core != self.half)
            def _():
                for j in range(N_T):
                    self.sib_copy(j).wait_send()

            @pl.when(core == self.half)
            def _():
                for yd in range(2):
                    for k in range(6):
                        self.z_copy(yd * 4, k).wait_send()

    q0 = Quarter(0, False, 0)
    q1 = Quarter(2, False, 1)
    q2 = Quarter(1, True, 2)
    q3 = Quarter(3, False, 6)
    g_acc[...] = jnp.zeros_like(g_acc)
    tgt_copy.wait()
    q0.first()
    q2.first()
    q0.second()
    q1.first()
    q0.third()
    q1.second()
    q0.finish()
    q2.second()
    q3.first()
    q1.third()
    nrm_cross(1)
    q0.own()
    q0.near()
    q1.finish()
    q2.third()
    q0.near_use()
    q3.second()
    nrm_cross(2)
    q1.own()
    q0.next_use()
    q0.far()
    q0.far_use()
    q1.near()
    q1.near_use()
    q2.finish()
    q0.relay_near()
    q3.third()
    q0.last_use()
    q1.far()
    q1.next_use()
    q0.last()
    q2.own()
    q2.near()
    q1.far_use()
    q3.finish()
    q2.near_use()
    q2.far()
    q1.relay_near()
    q1.last_use()
    q0.relay_far()
    q3.own()
    q3.near()
    q2.next_use()
    q2.far_use()
    q1.last()
    q3.near_use()
    q3.far()
    nrm_cross(3)
    q2.relay_near()
    q2.last_use()
    q3.next_use()
    q3.far_use()
    q3.last_use()

    key = kv[0]
    tkey = kv[1]
    val = kv[2]
    tval = kv[3]
    g1 = stack_heads(g_acc[:SEQ]).astype(BF16)
    g2 = stack_heads(g_acc[SEQ:]).astype(BF16)
    p = prob[...]
    tp = tprob[...]
    dpr = mm_nt(g1, val)
    tdpr = mm_nt(g2, val) + mm_nt(g1, tval)
    tval_grad = mm_tn(jnp.concatenate([tp, p], axis=0), jnp.concatenate([g1, g2], axis=0))
    grd_g[d, :, QW + HD :] = tval_grad.astype(BF16)
    dpr = dpr - jnp.sum(p * dpr, axis=1, keepdims=True)
    tdpr = tdpr - jnp.sum(tp * dpr + p * tdpr, axis=1, keepdims=True)
    ds = (p * dpr).astype(BF16)
    tds = (tp * dpr + p * tdpr).astype(BF16)
    both = jnp.concatenate([tds, ds], axis=0)
    trk_grad = mm_tn(both, rot_q[...]) * scale
    trk_grad = trk_grad * cos1 - swap_halves(trk_grad) * sin1
    grd_g[d, :, QW : QW + HD] = trk_grad.astype(BF16)
    trq_grad = (mm(tds, key) + mm(ds, tkey)) * scale
    trq_grad = trq_grad * cos4 - swap_halves(trq_grad) * sin4
    for h in range(HEADS):
        grd_g[d, :, h * HD : (h + 1) * HD] = trq_grad[h * SEQ : (h + 1) * SEQ].astype(BF16)

    def gs_copy(ry, rz):
        b = dev(ry, 4 - rz, 0)
        return remote(
            grd_g.at[b], grd_g.at[b], gs_s.at[ry, rz], gs_r.at[ry, rz], dp=dev(0, 0, 1)
        )

    def gz_copy(ry, k, sender=True):
        step = (1, 3, 1, 3)[k]
        back = (0, 0, 1, 1)[k] if sender else (1, 1, 2, 2)[k]
        b = dev(ry, 4 - back if step == 1 else back, 0)
        h = SEQ // 2
        rows = (pl.ds(0, SEQ), pl.ds(0, SEQ), pl.ds(0, h), pl.ds(h, h))[k]
        ref = grd_g.at[b, rows]
        return remote(ref, ref, gz_s.at[ry, k], gz_r.at[ry, k], dp=dev(0, step, 0))

    def gy_copy(b):
        return remote(grd_g.at[b], grd_g.at[b], gy_s, gy_r, dp=dev(1, 0, 0))

    other = lax.rem(y_hi + 1, 2)

    def z_sum(yd, sub):
        for k in (2, 3, 4, 5):
            own = (q0, q2)[sub]
            own.z_copy(yd * 4, k).wait_recv()
        rows = slice(sub * W, (sub + 1) * W)
        total = wq[core * N_T + yd * 4 + z, rows].astype(F32)
        return total + zr[yd, 0, rows].astype(F32) + zr[yd, 1, rows].astype(F32)

    def y_copy(sub):
        rows = pl.ds(sub * W, W)
        return remote(
            wq.at[core * N_T + other * 4 + z, rows], yr.at[rows], y_s.at[sub], y_r.at[sub],
            dp=dev(1, 0, 0),
        )

    def out_cross(sub):
        wq[core * N_T + other * 4 + z, sub * W : (sub + 1) * W] = z_sum(other, sub).astype(BF16)
        y_copy(sub).start()

    gy_copy(d).start()
    gz_copy(0, 0).start()
    gz_copy(0, 1).start()
    gs_copy(0, 0).start()
    q1.relay_far()
    q2.last()
    out_cross(0)
    q3.relay_near()
    q3.last()
    q2.relay_far()
    gy_copy(dev(1, 0, 0)).wait_recv()
    gz_copy(1, 0).start()
    gz_copy(1, 1).start()
    gs_copy(1, 0).start()
    for ry in range(2):
        for k, rz in ((0, 1), (1, 3)):
            gz_copy(ry, k, False).wait_recv()
            gz_copy(ry, k + 2).start()
            gs_copy(ry, rz).start()
        if ry == 0:
            q3.relay_far()

    out_cross(1)

    def product(first):
        rows = pl.ds(first * N_T, N_T)
        lhs = nrm_g[rows].reshape(N_T * SEQ, C)
        rhs = grd_g[rows].reshape(N_T * SEQ, QW + 2 * HD)
        return mm_tn(lhs, rhs)

    def arrived(ry):
        for rz in range(4):
            for rc in range(2):
                if (ry, rz, rc) != (0, 0, 0):
                    src = dev(ry, 4 - rz, rc)
                    r = (ry * 4 + rz) * 2 + rc
                    remote(
                        nrm_g.at[src], nrm_g.at[src], nrm_s.at[r], nrm_r.at[r], dp=src
                    ).wait_recv()
            b = dev(ry, 4 - rz, 1)
            remote(
                grd_g.at[b], grd_g.at[b], gs_s.at[ry, rz], gs_r.at[ry, rz], dp=dev(0, 0, 1)
            ).wait_recv()

    gz_copy(0, 2, False).wait_recv()
    gz_copy(0, 3, False).wait_recv()
    gs_copy(0, 2).start()
    for sub in range(2):
        ho[sub * W : (sub + 1) * W, :] = z_sum(y_hi, sub)
    arrived(0)
    out = product(y_hi)
    hq[...] = out[:, :QW]
    hk[...] = out[:, QW : QW + HD]
    hv[...] = out[:, QW + HD :]
    gz_copy(1, 2, False).wait_recv()
    gz_copy(1, 3, False).wait_recv()
    gs_copy(1, 2).start()
    for sub in range(2):
        y_copy(sub).wait_recv()
    ho[...] += yr[...].astype(F32)
    arrived(1)
    out = product(other)
    hq[...] += out[:, :QW]
    hk[...] += out[:, QW : QW + HD]
    hv[...] += out[:, QW + HD :]

    for rel in everyone:
        nrm_copy(*rel).wait_send()

    for quarter in (q0, q1, q2, q3):
        quarter.wait_sends()
    for yd in range(2):
        for k in range(4):
            gz_copy(yd, k).wait_send()
        for rz in range(4):
            gs_copy(yd, rz).wait_send()
        y_copy(yd).wait_send()
    gy_copy(d).wait_send()


def hand_over(a, b, c, e, a_out, b_out, c_out, e_out, a_buf, b_buf, c_buf, e_buf, sem):
    arrays = ((a, a_buf, a_out), (e, e_buf, e_out), (b, b_buf, b_out), (c, c_buf, c_out))
    loads, stores = [], []
    for i, (src, buf, dst) in enumerate(arrays):
        for part in range(2):
            rows = pl.ds(part * (C // 2), C // 2)
            loads.append(
                pltpu.make_async_copy(src.at[rows], buf.at[rows], sem.at[0, 2 * i + part])
            )
            stores.append(
                pltpu.make_async_copy(buf.at[rows], dst.at[rows], sem.at[1, 2 * i + part])
            )
    for load in loads:
        load.start()
    for load, store in zip(loads, stores):
        load.wait()
        store.start()
    for store in stores:
        store.wait()


def tables():
    frequency = np.exp(
        np.float32(-math.log(10000.0)) * np.arange(HD // 2, dtype=np.float32) * np.float32(2.0)
        / np.float32(HD)
    ).astype(np.float32)
    angles = np.arange(SEQ, dtype=np.float32)[:, None] * frequency[None, :]
    cosine = np.cos(angles).astype(np.float32)
    sine = np.sin(angles).astype(np.float32)
    return np.concatenate([cosine, cosine], 1), np.concatenate([-sine, sine], 1)


def local(
    tokens, target, norm_gain, w_query, w_key, w_value, w_out, t_query, t_key, t_value, t_out
):
    cos_t, sin_t = tables()
    any_spec = pl.BlockSpec(memory_space=pl.ANY)
    vmem = pl.BlockSpec(memory_space=pltpu.VMEM)
    dma = pltpu.SemaphoreType.DMA
    block = (2 * SEQ, C // 2)
    scratch = [
        pltpu.VMEM((SEQ, D), BF16),
        pltpu.VMEM((SEQ, 2 * C), BF16),
        pltpu.VMEM((N_DP, C, QW), BF16),
        pltpu.VMEM((N_DP, C, HD), BF16),
        pltpu.VMEM((N_DP, C, HD), BF16),
        pltpu.VMEM((N_DP, QW, C), BF16),
        pltpu.VMEM((N_DP, SEQ, C), BF16),
        pltpu.VMEM((N_DP, SEQ, C), BF16),
        pltpu.VMEM((2 * SEQ, QW), BF16),
        pltpu.VMEM((N_T, C, QW), BF16),
        pltpu.VMEM((2, 2, 2, SEQ, QW), BF16),
        pltpu.VMEM((2, 2, C, QW), BF16),
        pltpu.VMEM((C, QW), BF16),
        pltpu.VMEM((N_DP, SEQ, QW + 2 * HD), BF16),
        pltpu.VMEM((4, 2, 4) + block, BF16),
        pltpu.VMEM((4, 2, 2, SEQ, C // 2), BF16),
        pltpu.VMEM((4, 2, 2) + block, BF16),
        pltpu.VMEM((7,) + block, BF16),
        pltpu.VMEM((4, N_T) + block, BF16),
        pltpu.VMEM((2 * SEQ, QW), F32),
        pltpu.VMEM((SEQ, QW + 2 * HD), F32),
        pltpu.VMEM((HEADS * SEQ, SEQ), F32),
        pltpu.VMEM((HEADS * SEQ, SEQ), F32),
        pltpu.VMEM((2 * HEADS * SEQ, HD), BF16),
        pltpu.VMEM((4, SEQ, HD), BF16),
        dma((2,)), dma((3, N_DP)), dma((N_DP,)),
        dma((N_DP,)), dma((N_DP,)), dma((N_T, 2)), dma((N_T, 2)), dma((2, 2, 6)), dma((2, 2, 6)),
        dma((2,)), dma((2,)), dma((2, 4)), dma((2, 4)), dma, dma, dma((2, 4)), dma((2, 4)),
        dma((4, 2, 6)), dma((4, 2, 6)), dma((7,)), dma((7,)), dma((4, 9)), dma((4, 9)),
    ]
    shapes = tuple(jax.ShapeDtypeStruct((C, n), F32) for n in (QW, HD, HD, QW))
    results = pl.pallas_call(
        kernel,
        out_shape=shapes,
        in_specs=[
            any_spec, any_spec, vmem, any_spec, any_spec, any_spec, any_spec,
            vmem, vmem, vmem, vmem, vmem, vmem,
        ],
        out_specs=(vmem, vmem, vmem, vmem),
        scratch_shapes=scratch,
        compiler_params=pltpu.CompilerParams(
            collective_id=0, has_side_effects=True, vmem_limit_bytes=62 * 1024 * 1024
        ),
        cost_estimate=pl.CostEstimate(
            flops=10_000_000_000, bytes_accessed=26_000_000, transcendentals=65536
        ),
        name="hvp",
    )(
        tokens, target, norm_gain.reshape(1, D), w_query, w_key, w_value, w_out,
        t_query.reshape(1, QW), t_key.reshape(1, HD), t_value.reshape(1, HD),
        t_out.reshape(1, D), jnp.asarray(cos_t), jnp.asarray(sin_t),
    )
    return pl.pallas_call(
        hand_over,
        out_shape=shapes,
        in_specs=[any_spec] * 4,
        out_specs=(any_spec,) * 4,
        scratch_shapes=[pltpu.VMEM((C, n), F32) for n in (QW, HD, HD, QW)] + [dma((2, 8))],
        compiler_params=pltpu.CompilerParams(vmem_limit_bytes=62 * 1024 * 1024),
        name="results",
    )(*results)


def solution(mesh):
    return jax.shard_map(
        local,
        mesh=mesh,
        in_specs=(
            P("dp", None),
            P("dp", None),
            P(),
            P(None, "tensor"),
            P(None, "tensor"),
            P(None, "tensor"),
            P("tensor", None),
            P("tensor"),
            P("tensor"),
            P("tensor"),
            P(),
        ),
        out_specs=(P("dp", "tensor"), P("dp", "tensor"), P("dp", "tensor"), P("dp", "tensor")),
        check_vma=False,
    )
```

time: 140 us -> 125 us (0.89)
  the two profiles are of different devices: /device:TPU:20 before, /device:TPU:13 now
where the time goes in v4:
time: 125 us
  Pallas kernels  124 us (99%)
    pallas_call x1, Pallas kernels, local(): pl.pallas_call(kernel, out_shape=shapes, in_specs=[any_spec, any_spec, vm...  121 us
    pallas_call x1, Pallas kernels, local(): pl.pallas_call(hand_over, out_shape=shapes, in_specs=[any_spec] * 4, out_...  2.66 us

profile of v4, /device:TPU:13, one launch (start us, length us, event | category | flops | bytes accessed | tf_op | source)
XLA Modules:
  0.0 124.8 jit_solution(3393134827279079332)
XLA Ops:
  0.6 121.3 %hvp.1 = (f32[512,512]{1,0:T(8,128)}, f32[512,128]{1,0:T(8,128)}, f32[512,128]{1,0:T(8,128)}, f32[512,512]{1,0:T(8,128)}) custom-call(bf16[128,8192]{1,0:T(8,128)(2,1)} %tok_hbm.1, bf16[128,8192]{1,0:T(8,128)(2,1)} %tgt_hbm.1, f32[1,8192]{1,0:T(1,128)} %bitcast.5, bf16[8192,512]{1,0:T(8,128)(2,1)} %wq_hbm.1, bf16[8192,128]{1,0:T(8,128)(2,1)} %wk_hbm.1, ...), custom_call_target="tpu_custom_call" | custom-call | flops 10000000000 | bytes 26000000 | tf_op jit(solution)/shard_map/hvp/pallas_call | solution.py:761
  122.0 2.7 %results.1 = (f32[512,512]{1,0:T(8,128)}, f32[512,128]{1,0:T(8,128)}, f32[512,128]{1,0:T(8,128)}, f32[512,512]{1,0:T(8,128)}) custom-call(f32[512,512]{1,0:T(8,128)} %get-tuple-element.8.a, f32[512,128]{1,0:T(8,128)} %get-tuple-element.9.b, f32[512,128]{1,0:T(8,128)} %get-tuple-element.10.c, f32[512,512]{1,0:T(8,128)} %get-tuple-element.11.e), custom_call_target="tpu_custom_call" | custom-call | tf_op jit(solution)/shard_map/results/pallas_call | solution.py:782

commit v5 on v4

--- a/solution.py
+++ b/solution.py
@@ -59,14 +59,14 @@
 
 def kernel(
     tok_hbm, tgt_hbm, gain, wq_hbm, wk_hbm, wv_hbm, wo_hbm, tq, tk, tv, t_out, cos_t, sin_t,
-    hq, hk, hv, ho,
-    tok, tgt, wq, wk, wv, wo, nrm, nrm_g, att, sib, zf, zr, yr, grd_g,
+    hq_hbm, hk_hbm, hv_hbm, ho_hbm,
+    hq, hk, hv, ho, tok, tgt, wq, wk, wv, wo, nrm, nrm_g, att, sib, zf, zr, yr, grd_g, gkv_g,
     pq, pf, pv, pc, r_all, g_acc, proj,
     prob, tprob, rot_q, kv,
-    in_sem, wqkv_sem, wo_sem,
+    in_sem, out_sem, wqkv_sem, wo_sem,
     nrm_s, nrm_r, sib_s, sib_r, z_s, z_r, y_s, y_r,
-    gz_s, gz_r, gy_s, gy_r, gs_s, gs_r,
-    rs_s, rs_r, cr_s, cr_r, ga_s, ga_r,
+    gz_s, gz_r, gy_r, gs_s, gs_r, hz_s, hz_r, hy_r, hs_s, hs_r,
+    rs_s, rs_r, cr_r, ga_s, ga_r,
 ):
     d = lax.axis_index("dp")
     t = lax.axis_index("tensor")
@@ -88,28 +88,40 @@
             device_id=where, device_id_type=MESH,
         )
 
+    bar = pltpu.get_barrier_semaphore()
+
+    @pl.loop(1, N_DP)
+    def _(r):
+        pl.semaphore_signal(
+            bar, inc=1, device_id={"dp": lax.rem(d + r, N_DP)}, device_id_type=MESH
+        )
+
+    for dy, dx in ((1, 0), (0, 1), (0, 2), (0, 3)):
+        pl.semaphore_signal(bar, inc=1, device_id={"tensor": at(dy, dx)}, device_id_type=MESH)
+
     tok_copy = pltpu.make_async_copy(tok_hbm, tok, in_sem.at[0])
     tok_copy.start()
     tgt_copy = pltpu.make_async_copy(
         tgt_hbm.at[:, pl.ds(pl.multiple_of(t * 2 * C, 2 * C), 2 * C)], tgt, in_sem.at[1]
     )
 
-    def w_copies(c):
-        rows = pl.ds(c * C, C)
-        return (
-            pltpu.make_async_copy(wq_hbm.at[rows, :], wq.at[c], wqkv_sem.at[0, c]),
-            pltpu.make_async_copy(wk_hbm.at[rows, :], wk.at[c], wqkv_sem.at[1, c]),
-            pltpu.make_async_copy(wv_hbm.at[rows, :], wv.at[c], wqkv_sem.at[2, c]),
-        )
+    GROUP = 4
+
+    def w_copies(g):
+        part = pl.ds(g * GROUP, GROUP)
+        return [
+            pltpu.make_async_copy(src.at[part], dst.at[part], wqkv_sem.at[i, g])
+            for i, (src, dst) in enumerate(((wq_hbm, wq), (wk_hbm, wk), (wv_hbm, wv)))
+        ]
 
     def wo_copy(c):
         return pltpu.make_async_copy(
-            wo_hbm.at[:, pl.ds(pl.multiple_of(c * C, C), C)], wo.at[c], wo_sem.at[c]
+            wo_hbm.at[:, pl.ds(pl.multiple_of(c * C, C), C)], wo.at[c], wo_sem
         )
 
-    @pl.loop(0, N_DP)
-    def _(c):
-        for cp in w_copies(c):
+    @pl.loop(0, N_DP // GROUP)
+    def _(g):
+        for cp in w_copies(g):
             cp.start()
 
     tgt_copy.start()
@@ -117,17 +129,6 @@
     @pl.loop(0, N_DP)
     def _(c):
         wo_copy(c).start()
-
-    bar = pltpu.get_barrier_semaphore()
-
-    @pl.loop(1, N_DP)
-    def _(r):
-        pl.semaphore_signal(
-            bar, inc=1, device_id={"dp": lax.rem(d + r, N_DP)}, device_id_type=MESH
-        )
-
-    for dy, dx in ((1, 0), (0, 1), (0, 2), (0, 3)):
-        pl.semaphore_signal(bar, inc=1, device_id={"tensor": at(dy, dx)}, device_id_type=MESH)
 
     tok_copy.wait()
 
@@ -150,7 +151,7 @@
     def nrm_copy(ry, rz, rc):
         dest = dev(ry, rz, rc)
         r = (ry * 4 + rz) * 2 + rc
-        return remote(nrm.at[dest], nrm_g.at[d], nrm_s.at[r], nrm_r.at[r], dp=dest)
+        return remote(nrm.at[dest], nrm_g.at[d], nrm_s, nrm_r.at[r], dp=dest)
 
     early = [(0, rz, rc) for rz in (1, 3, 2) for rc in (0, 1)] + [(0, 0, 1)]
     crossing = [[(1, rz, rc) for rc in (0, 1)] for rz in (2, 1, 3, 0)]
@@ -164,16 +165,23 @@
         nrm_copy(*rel).start()
     nrm_cross(0)
 
-    proj[...] = jnp.zeros_like(proj)
-
-    @pl.loop(0, N_DP)
-    def _(c):
-        for cp in w_copies(c):
+    @pl.loop(0, N_DP // GROUP)
+    def _(g):
+        total = [jnp.zeros((SEQ, n), F32) for n in (QW, HD, HD)]
+        for cp in w_copies(g):
             cp.wait()
-        lhs = nrm[c]
-        proj[:, :QW] += mm(lhs, wq[c])
-        proj[:, QW : QW + HD] += mm(lhs, wk[c])
-        proj[:, QW + HD :] += mm(lhs, wv[c])
+        for i in range(GROUP):
+            c = g * GROUP + i
+            lhs = nrm[c]
+            total = [a + mm(lhs, w[c]) for a, w in zip(total, (wq, wk, wv))]
+
+        @pl.when(g == 0)
+        def _():
+            proj[...] = jnp.concatenate(total, axis=1)
+
+        @pl.when(g > 0)
+        def _():
+            proj[...] += jnp.concatenate(total, axis=1)
 
     cos1 = cos_t[...]
     sin1 = sin_t[...]
@@ -213,9 +221,7 @@
         att[:SEQ, h * HD : (h + 1) * HD] = to[h * SEQ : (h + 1) * SEQ].astype(BF16)
         att[SEQ:, h * HD : (h + 1) * HD] = o[h * SEQ : (h + 1) * SEQ].astype(BF16)
 
-    @pl.loop(0, N_DP)
-    def _(c):
-        wo_copy(c).wait()
+    pltpu.make_async_copy(wo, wo, wo_sem).wait()
 
     W = C // 2
 
@@ -239,14 +245,14 @@
             side = 0 if step == 1 else 1
             dst = pf.at[self.q, dy, side] if k < 2 else pv.at[self.q, dy, side, rows]
             return remote(
-                pq.at[self.q, dy, dx, rows], dst, rs_s.at[self.q, dy, k], rs_r.at[self.q, dy, k],
+                pq.at[self.q, dy, dx, rows], dst, rs_s.at[self.q], rs_r.at[self.q, dy, k],
                 tensor=at(0, step),
             )
 
         def cross(self, dx):
             slot = self.base + dx
             return remote(
-                pq.at[self.q, 1, dx], pc.at[slot], cr_s.at[slot], cr_r.at[slot], tensor=at(1, 0)
+                pq.at[self.q, 1, dx], pc.at[slot], rs_s.at[self.q], cr_r.at[slot], tensor=at(1, 0)
             )
 
         def add(self, dx, rows, dy, value):
@@ -286,7 +292,7 @@
                 ref = r_all.at[self.q, j, pl.ds(0, SEQ)]
             if k in upper:
                 ref = r_all.at[self.q, j, pl.ds(SEQ, SEQ)]
-            return remote(ref, ref, ga_s.at[self.q, k], ga_r.at[self.q, k], tensor=to[k])
+            return remote(ref, ref, ga_s.at[self.q], ga_r.at[self.q, k], tensor=to[k])
 
         def came(self, *ks):
             for k in ks:
@@ -344,7 +350,7 @@
         def sib_copy(self, j):
             rows = pl.ds(self.sub * W, W)
             return remote(
-                wq.at[self.half * N_T + j, rows], sib.at[j, rows], sib_s.at[j, self.sub],
+                wq.at[self.half * N_T + j, rows], sib.at[j, rows], sib_s.at[self.sub],
                 sib_r.at[j, self.sub], dp=dev(0, 0, 1),
             )
 
@@ -369,7 +375,7 @@
             side = 0 if step == 1 else 1
             dst = zf.at[self.sub, yd, side] if k < 2 else zr.at[yd, side, rows]
             return remote(
-                wq.at[self.half * N_T + j, rows], dst, z_s.at[self.sub, yd, k],
+                wq.at[self.half * N_T + j, rows], dst, z_s.at[self.sub],
                 z_r.at[self.sub, yd, k], dp=dev(0, step, 0),
             )
 
@@ -428,23 +434,25 @@
         def own(self):
             self.use(t)
 
+        def own_sum(self):
+            self.combine(t)
+
         def near_use(self):
             self.use(at(0, 3), at(0, 1))
-            self.combine(t)
             if self.y_first:
                 self.came(0)
             self.use(at(1, 0))
 
         def next_use(self):
+            self.combine(at(0, 3), at(0, 1), at(1, 0))
             if not self.y_first:
                 self.came(3, 4)
-            self.combine(at(0, 3), at(0, 1))
             self.use(at(0, 2))
 
         def far_use(self):
             if self.y_first:
                 self.came(5, 6)
-            self.combine(at(1, 0), at(0, 2))
+            self.combine(at(0, 2))
             self.use(at(1, 3), at(1, 1))
 
         def last_use(self):
@@ -460,32 +468,51 @@
             self.z_relay(at(1, 0), at(0, 2))
 
         def relay_far(self):
-            self.z_relay(at(1, 3), at(1, 1), at(1, 2))
+            self.z_relay(at(1, 3), at(1, 1))
+
+        def relay_last(self):
+            self.z_relay(at(1, 2))
 
         def wait_sends(self):
-            for dy in (0,) if self.y_first else (0, 1):
-                for k in range(6):
-                    self.ring(dy, k).wait_send()
-            for dx in range(4) if self.y_first else (0,):
-                self.cross(dx).wait_send()
-            for k in range(8 if self.y_first else 9):
-                self.gather(k).wait_send()
+            sent = r_all.at[self.q, pl.ds(0, 7)]
+            pltpu.make_async_copy(sent, sent, rs_s.at[self.q]).wait()
+            pltpu.make_async_copy(sent, sent, ga_s.at[self.q]).wait()
 
             @pl.when(core != self.half)
             def _():
-                for j in range(N_T):
-                    self.sib_copy(j).wait_send()
+                to_core = wq.at[pl.ds(0, 4)]
+                pltpu.make_async_copy(to_core, to_core, sib_s.at[self.sub]).wait()
 
             @pl.when(core == self.half)
             def _():
-                for yd in range(2):
-                    for k in range(6):
-                        self.z_copy(yd * 4, k).wait_send()
+                along_z = wq.at[pl.ds(0, 3)]
+                pltpu.make_async_copy(along_z, along_z, z_s.at[self.sub]).wait()
 
     q0 = Quarter(0, False, 0)
     q1 = Quarter(2, False, 1)
     q2 = Quarter(1, True, 2)
     q3 = Quarter(3, False, 6)
+    other = lax.rem(y_hi + 1, 2)
+
+    def z_sum(yd, sub):
+        for k in (2, 3, 4, 5):
+            own = (q0, q2)[sub]
+            own.z_copy(yd * 4, k).wait_recv()
+        rows = slice(sub * W, (sub + 1) * W)
+        total = wq[core * N_T + yd * 4 + z, rows].astype(F32)
+        return total + zr[yd, 0, rows].astype(F32) + zr[yd, 1, rows].astype(F32)
+
+    def y_copy(sub):
+        rows = pl.ds(sub * W, W)
+        return remote(
+            wq.at[core * N_T + other * 4 + z, rows], yr.at[rows], y_s.at[sub], y_r.at[sub],
+            dp=dev(1, 0, 0),
+        )
+
+    def out_cross(sub):
+        wq[core * N_T + other * 4 + z, sub * W : (sub + 1) * W] = z_sum(other, sub).astype(BF16)
+        y_copy(sub).start()
+
     g_acc[...] = jnp.zeros_like(g_acc)
     tgt_copy.wait()
     q0.first()
@@ -502,43 +529,52 @@
     q0.own()
     q0.near()
     q1.finish()
+    q1.own()
     q2.third()
+    q0.own_sum()
     q0.near_use()
     q3.second()
     nrm_cross(2)
-    q1.own()
+    q1.own_sum()
     q0.next_use()
     q0.far()
     q0.far_use()
     q1.near()
     q1.near_use()
     q2.finish()
+    q2.own()
     q0.relay_near()
     q3.third()
     q0.last_use()
+    q2.own_sum()
+    q0.last()
     q1.far()
     q1.next_use()
-    q0.last()
-    q2.own()
     q2.near()
     q1.far_use()
     q3.finish()
+    q3.own()
     q2.near_use()
+    q0.relay_far()
     q2.far()
+    q3.own_sum()
     q1.relay_near()
     q1.last_use()
-    q0.relay_far()
-    q3.own()
+    q0.relay_last()
     q3.near()
     q2.next_use()
+    q1.last()
     q2.far_use()
-    q1.last()
     q3.near_use()
+    q1.relay_far()
     q3.far()
     nrm_cross(3)
     q2.relay_near()
     q2.last_use()
     q3.next_use()
+    q2.last()
+    q1.relay_last()
+    out_cross(0)
     q3.far_use()
     q3.last_use()
 
@@ -553,7 +589,7 @@
     dpr = mm_nt(g1, val)
     tdpr = mm_nt(g2, val) + mm_nt(g1, tval)
     tval_grad = mm_tn(jnp.concatenate([tp, p], axis=0), jnp.concatenate([g1, g2], axis=0))
-    grd_g[d, :, QW + HD :] = tval_grad.astype(BF16)
+    gkv_g[d, :, HD:] = tval_grad.astype(BF16)
     dpr = dpr - jnp.sum(p * dpr, axis=1, keepdims=True)
     tdpr = tdpr - jnp.sum(tp * dpr + p * tdpr, axis=1, keepdims=True)
     ds = (p * dpr).astype(BF16)
@@ -561,7 +597,7 @@
     both = jnp.concatenate([tds, ds], axis=0)
     trk_grad = mm_tn(both, rot_q[...]) * scale
     trk_grad = trk_grad * cos1 - swap_halves(trk_grad) * sin1
-    grd_g[d, :, QW : QW + HD] = trk_grad.astype(BF16)
+    gkv_g[d, :, :HD] = trk_grad.astype(BF16)
     trq_grad = (mm(tds, key) + mm(ds, tkey)) * scale
     trq_grad = trq_grad * cos4 - swap_halves(trq_grad) * sin4
     for h in range(HEADS):
@@ -570,7 +606,7 @@
     def gs_copy(ry, rz):
         b = dev(ry, 4 - rz, 0)
         return remote(
-            grd_g.at[b], grd_g.at[b], gs_s.at[ry, rz], gs_r.at[ry, rz], dp=dev(0, 0, 1)
+            grd_g.at[b], grd_g.at[b], gs_s, gs_r.at[ry, rz], dp=dev(0, 0, 1)
         )
 
     def gz_copy(ry, k, sender=True):
@@ -580,61 +616,77 @@
         h = SEQ // 2
         rows = (pl.ds(0, SEQ), pl.ds(0, SEQ), pl.ds(0, h), pl.ds(h, h))[k]
         ref = grd_g.at[b, rows]
-        return remote(ref, ref, gz_s.at[ry, k], gz_r.at[ry, k], dp=dev(0, step, 0))
+        return remote(ref, ref, gz_s, gz_r.at[ry, k], dp=dev(0, step, 0))
 
     def gy_copy(b):
-        return remote(grd_g.at[b], grd_g.at[b], gy_s, gy_r, dp=dev(1, 0, 0))
-
-    other = lax.rem(y_hi + 1, 2)
-
-    def z_sum(yd, sub):
-        for k in (2, 3, 4, 5):
-            own = (q0, q2)[sub]
-            own.z_copy(yd * 4, k).wait_recv()
-        rows = slice(sub * W, (sub + 1) * W)
-        total = wq[core * N_T + yd * 4 + z, rows].astype(F32)
-        return total + zr[yd, 0, rows].astype(F32) + zr[yd, 1, rows].astype(F32)
-
-    def y_copy(sub):
-        rows = pl.ds(sub * W, W)
+        return remote(grd_g.at[b], grd_g.at[b], gz_s, gy_r, dp=dev(1, 0, 0))
+
+    def hs_copy(ry, rz):
+        b = dev(ry, 4 - rz, 0)
         return remote(
-            wq.at[core * N_T + other * 4 + z, rows], yr.at[rows], y_s.at[sub], y_r.at[sub],
-            dp=dev(1, 0, 0),
+            gkv_g.at[b], gkv_g.at[b], hs_s, hs_r.at[ry, rz], dp=dev(0, 0, 1)
         )
 
-    def out_cross(sub):
-        wq[core * N_T + other * 4 + z, sub * W : (sub + 1) * W] = z_sum(other, sub).astype(BF16)
-        y_copy(sub).start()
+    def hz_copy(k, sender=True):
+        step = (1, 3, 1, 3)[k]
+        back = (0, 0, 1, 1)[k] if sender else (1, 1, 2, 2)[k]
+        b = dev(0, 4 - back if step == 1 else back, 0)
+        h = SEQ // 2
+        rows = (pl.ds(0, SEQ), pl.ds(0, SEQ), pl.ds(0, h), pl.ds(h, h))[k]
+        ref = gkv_g.at[b, rows]
+        return remote(ref, ref, hz_s, hz_r.at[k], dp=dev(0, step, 0))
+
+    def hy_copy(rz, sender=True):
+        b = dev(0 if sender else 1, 4 - rz, 0)
+        return remote(gkv_g.at[b], gkv_g.at[b], hz_s, hy_r.at[rz], dp=dev(1, 0, 0))
+
+    def pass_on(ry):
+        for k, rz in ((0, 1), (1, 3)):
+            gz_copy(ry, k, False).wait_recv()
+            gz_copy(ry, k + 2).start()
+            gs_copy(ry, rz).start()
 
     gy_copy(d).start()
+    hy_copy(0).start()
+    hz_copy(0).start()
+    hz_copy(1).start()
     gz_copy(0, 0).start()
     gz_copy(0, 1).start()
+    hs_copy(0, 0).start()
     gs_copy(0, 0).start()
-    q1.relay_far()
-    q2.last()
-    out_cross(0)
     q3.relay_near()
     q3.last()
     q2.relay_far()
+    q2.relay_last()
+    for k, rz in ((0, 1), (1, 3)):
+        hz_copy(k, False).wait_recv()
+        hz_copy(k + 2).start()
+        hy_copy(rz).start()
+        hs_copy(0, rz).start()
     gy_copy(dev(1, 0, 0)).wait_recv()
     gz_copy(1, 0).start()
     gz_copy(1, 1).start()
     gs_copy(1, 0).start()
-    for ry in range(2):
-        for k, rz in ((0, 1), (1, 3)):
-            gz_copy(ry, k, False).wait_recv()
-            gz_copy(ry, k + 2).start()
-            gs_copy(ry, rz).start()
-        if ry == 0:
-            q3.relay_far()
-
+    q3.relay_far()
+    pass_on(0)
+    q3.relay_last()
+    hz_copy(2, False).wait_recv()
+    hz_copy(3, False).wait_recv()
+    hy_copy(2).start()
+    hs_copy(0, 2).start()
+    hy_copy(0, False).wait_recv()
+    hs_copy(1, 0).start()
     out_cross(1)
+    pass_on(1)
+    for rz in (1, 3):
+        hy_copy(rz, False).wait_recv()
+        hs_copy(1, rz).start()
 
     def product(first):
         rows = pl.ds(first * N_T, N_T)
         lhs = nrm_g[rows].reshape(N_T * SEQ, C)
-        rhs = grd_g[rows].reshape(N_T * SEQ, QW + 2 * HD)
-        return mm_tn(lhs, rhs)
+        of_query = mm_tn(lhs, grd_g[rows].reshape(N_T * SEQ, QW))
+        return of_query, mm_tn(lhs, gkv_g[rows].reshape(N_T * SEQ, 2 * HD))
 
     def arrived(ry):
         for rz in range(4):
@@ -643,11 +695,14 @@
                     src = dev(ry, 4 - rz, rc)
                     r = (ry * 4 + rz) * 2 + rc
                     remote(
-                        nrm_g.at[src], nrm_g.at[src], nrm_s.at[r], nrm_r.at[r], dp=src
+                        nrm_g.at[src], nrm_g.at[src], nrm_s, nrm_r.at[r], dp=src
                     ).wait_recv()
             b = dev(ry, 4 - rz, 1)
             remote(
-                grd_g.at[b], grd_g.at[b], gs_s.at[ry, rz], gs_r.at[ry, rz], dp=dev(0, 0, 1)
+                grd_g.at[b], grd_g.at[b], gs_s, gs_r.at[ry, rz], dp=dev(0, 0, 1)
+            ).wait_recv()
+            remote(
+                gkv_g.at[b], gkv_g.at[b], hs_s, hs_r.at[ry, rz], dp=dev(0, 0, 1)
             ).wait_recv()
 
     gz_copy(0, 2, False).wait_recv()
@@ -656,34 +711,46 @@
     for sub in range(2):
         ho[sub * W : (sub + 1) * W, :] = z_sum(y_hi, sub)
     arrived(0)
-    out = product(y_hi)
-    hq[...] = out[:, :QW]
-    hk[...] = out[:, QW : QW + HD]
-    hv[...] = out[:, QW + HD :]
+    of_query, of_kv = product(y_hi)
+    hq[...] = of_query
+    hk[...] = of_kv[:, :HD]
+    hv[...] = of_kv[:, HD:]
     gz_copy(1, 2, False).wait_recv()
     gz_copy(1, 3, False).wait_recv()
     gs_copy(1, 2).start()
+    hy_copy(2, False).wait_recv()
+    hs_copy(1, 2).start()
     for sub in range(2):
         y_copy(sub).wait_recv()
+
+    def stores(i):
+        src, dst = ((hq, hq_hbm), (hk, hk_hbm), (hv, hv_hbm), (ho, ho_hbm))[i]
+        return [pltpu.make_async_copy(src, dst, out_sem.at[i])]
+
     ho[...] += yr[...].astype(F32)
+    for cp in stores(3):
+        cp.start()
     arrived(1)
-    out = product(other)
-    hq[...] += out[:, :QW]
-    hk[...] += out[:, QW : QW + HD]
-    hv[...] += out[:, QW + HD :]
-
-    for rel in everyone:
-        nrm_copy(*rel).wait_send()
+    of_query, of_kv = product(other)
+    hq[...] += of_query
+    hk[...] += of_kv[:, :HD]
+    hv[...] += of_kv[:, HD:]
+    for i in (0, 1, 2):
+        for cp in stores(i):
+            cp.start()
 
     for quarter in (q0, q1, q2, q3):
         quarter.wait_sends()
-    for yd in range(2):
-        for k in range(4):
-            gz_copy(yd, k).wait_send()
-        for rz in range(4):
-            gs_copy(yd, rz).wait_send()
-        y_copy(yd).wait_send()
-    gy_copy(d).wait_send()
+    for sub in range(2):
+        y_copy(sub).wait_send()
+    for ref, blocks, sem in (
+        (nrm_g, N_DP - 1, nrm_s), (grd_g, 7, gz_s), (grd_g, 8, gs_s), (gkv_g, 7, hz_s), (gkv_g, 8, hs_s),
+    ):
+        sent = ref.at[pl.ds(0, blocks)]
+        pltpu.make_async_copy(sent, sent, sem).wait()
+    for i in range(4):
+        for cp in stores(i):
+            cp.wait()
 
 
 def hand_over(a, b, c, e, a_out, b_out, c_out, e_out, a_buf, b_buf, c_buf, e_buf, sem):
@@ -727,6 +794,10 @@
     dma = pltpu.SemaphoreType.DMA
     block = (2 * SEQ, C // 2)
     scratch = [
+        pltpu.VMEM((C, QW), F32),
+        pltpu.VMEM((C, HD), F32),
+        pltpu.VMEM((C, HD), F32),
+        pltpu.VMEM((C, QW), F32),
         pltpu.VMEM((SEQ, D), BF16),
         pltpu.VMEM((SEQ, 2 * C), BF16),
         pltpu.VMEM((N_DP, C, QW), BF16),
@@ -740,7 +811,8 @@
         pltpu.VMEM((2, 2, 2, SEQ, QW), BF16),
         pltpu.VMEM((2, 2, C, QW), BF16),
         pltpu.VMEM((C, QW), BF16),
-        pltpu.VMEM((N_DP, SEQ, QW + 2 * HD), BF16),
+        pltpu.VMEM((N_DP, SEQ, QW), BF16),
+        pltpu.VMEM((N_DP, SEQ, 2 * HD), BF16),
         pltpu.VMEM((4, 2, 4) + block, BF16),
         pltpu.VMEM((4, 2, 2, SEQ, C // 2), BF16),
         pltpu.VMEM((4, 2, 2) + block, BF16),
@@ -752,10 +824,10 @@
         pltpu.VMEM((HEADS * SEQ, SEQ), F32),
         pltpu.VMEM((2 * HEADS * SEQ, HD), BF16),
         pltpu.VMEM((4, SEQ, HD), BF16),
-        dma((2,)), dma((3, N_DP)), dma((N_DP,)),
-        dma((N_DP,)), dma((N_DP,)), dma((N_T, 2)), dma((N_T, 2)), dma((2, 2, 6)), dma((2, 2, 6)),
-        dma((2,)), dma((2,)), dma((2, 4)), dma((2, 4)), dma, dma, dma((2, 4)), dma((2, 4)),
-        dma((4, 2, 6)), dma((4, 2, 6)), dma((7,)), dma((7,)), dma((4, 9)), dma((4, 9)),
+        dma((2,)), dma((4,)), dma((3, 4)), dma,
+        dma, dma((N_DP,)), dma((2,)), dma((N_T, 2)), dma((2,)), dma((2, 2, 6)), dma((2,)), dma((2,)),
+        dma, dma((2, 4)), dma, dma, dma((2, 4)), dma, dma((4,)), dma((4,)), dma, dma((2, 4)),
+        dma((4,)), dma((4, 2, 6)), dma((7,)), dma((4,)), dma((4, 9)),
     ]
     shapes = tuple(jax.ShapeDtypeStruct((C, n), F32) for n in (QW, HD, HD, QW))
     results = pl.pallas_call(
@@ -765,7 +837,7 @@
             any_spec, any_spec, vmem, any_spec, any_spec, any_spec, any_spec,
             vmem, vmem, vmem, vmem, vmem, vmem,
         ],
-        out_specs=(vmem, vmem, vmem, vmem),
+        out_specs=(any_spec,) * 4,
         scratch_shapes=scratch,
         compiler_params=pltpu.CompilerParams(
             collective_id=0, has_side_effects=True, vmem_limit_bytes=62 * 1024 * 1024
@@ -775,7 +847,8 @@
         ),
         name="hvp",
     )(
-        tokens, target, norm_gain.reshape(1, D), w_query, w_key, w_value, w_out,
+        tokens, target, norm_gain.reshape(1, D), w_query.reshape(N_DP, C, QW),
+        w_key.reshape(N_DP, C, HD), w_value.reshape(N_DP, C, HD), w_out,
         t_query.reshape(1, QW), t_key.reshape(1, HD), t_value.reshape(1, HD),
         t_out.reshape(1, D), jnp.asarray(cos_t), jnp.asarray(sin_t),
     )

time: 125 us -> 116 us (0.928)
  Pallas kernels: 124 us -> 116 us
    pallas_call x1, Pallas kernels: 121 us -> 113 us  [local(): pl.pallas_call(kernel, out_shape=shapes, in_specs=[any_spec, any_spec, vm...]
where the time goes in v5:
time: 116 us
  Pallas kernels  116 us (100%)
    pallas_call x1, Pallas kernels, local(): pl.pallas_call(kernel, out_shape=shapes, in_specs=[any_spec, any_spec, vm...  113 us
    pallas_call x1, Pallas kernels, local(): pl.pallas_call(hand_over, out_shape=shapes, in_specs=[any_spec] * 4, out_...  2.66 us

profile of v5, /device:TPU:13, one launch (start us, length us, event | category | flops | bytes accessed | tf_op | source)
XLA Modules:
  0.0 116.3 jit_solution(5037062164092602305)
XLA Ops:
  0.6 112.8 %hvp.1 = (f32[512,512]{1,0:T(8,128)}, f32[512,128]{1,0:T(8,128)}, f32[512,128]{1,0:T(8,128)}, f32[512,512]{1,0:T(8,128)}) custom-call(bf16[128,8192]{1,0:T(8,128)(2,1)} %tok_hbm.1, bf16[128,8192]{1,0:T(8,128)(2,1)} %tgt_hbm.1, f32[1,8192]{1,0:T(1,128)} %bitcast.11, bf16[16,512,512]{2,1,0:T(8,128)(2,1)} %bitcast.8, bf16[16,512,128]{2,1,0:T(8,128)(2,1)} %bitcast.9, ...), custom_call_target="tpu_custom_call" | custom-call | flops 10000000000 | bytes 26000000 | tf_op jit(solution)/shard_map/hvp/pallas_call | solution.py:833
  113.5 2.7 %results.1 = (f32[512,512]{1,0:T(8,128)}, f32[512,128]{1,0:T(8,128)}, f32[512,128]{1,0:T(8,128)}, f32[512,512]{1,0:T(8,128)}) custom-call(f32[512,512]{1,0:T(8,128)} %get-tuple-element.8.a, f32[512,128]{1,0:T(8,128)} %get-tuple-element.9.b, f32[512,128]{1,0:T(8,128)} %get-tuple-element.10.c, f32[512,512]{1,0:T(8,128)} %get-tuple-element.11.e), custom_call_target="tpu_custom_call" | custom-call | tf_op jit(solution)/shard_map/results/pallas_call | solution.py:855

commit v6 on v5

--- a/solution.py
+++ b/solution.py
@@ -134,9 +134,10 @@
 
     def square_step(c, acc):
         v = tok[:, pl.ds(pl.multiple_of(c * C, C), C)].astype(F32)
-        return acc + v * v
-
-    squares = lax.fori_loop(0, N_DP, square_step, jnp.zeros((SEQ, C), F32))
+        v = v * v
+        return acc + ((v[:, :HD] + v[:, HD : 2 * HD]) + (v[:, 2 * HD : 3 * HD] + v[:, 3 * HD :]))
+
+    squares = lax.fori_loop(0, N_DP, square_step, jnp.zeros((SEQ, HD), F32))
     inv = lax.rsqrt(jnp.sum(squares, axis=1, keepdims=True) * (1.0 / D) + EPS)
 
     @pl.loop(0, N_DP)
@@ -150,8 +151,7 @@
 
     def nrm_copy(ry, rz, rc):
         dest = dev(ry, rz, rc)
-        r = (ry * 4 + rz) * 2 + rc
-        return remote(nrm.at[dest], nrm_g.at[d], nrm_s, nrm_r.at[r], dp=dest)
+        return remote(nrm.at[dest], nrm_g.at[d], nrm_s, nrm_r.at[ry], dp=dest)
 
     early = [(0, rz, rc) for rz in (1, 3, 2) for rc in (0, 1)] + [(0, 0, 1)]
     crossing = [[(1, rz, rc) for rc in (0, 1)] for rz in (2, 1, 3, 0)]
@@ -245,7 +245,7 @@
             side = 0 if step == 1 else 1
             dst = pf.at[self.q, dy, side] if k < 2 else pv.at[self.q, dy, side, rows]
             return remote(
-                pq.at[self.q, dy, dx, rows], dst, rs_s.at[self.q], rs_r.at[self.q, dy, k],
+                pq.at[self.q, dy, dx, rows], dst, rs_s.at[self.q], rs_r.at[self.q, dy, min(k, 2)],
                 tensor=at(0, step),
             )
 
@@ -268,8 +268,8 @@
             self.ring(dy, 5).start()
 
         def row_sum(self, dy):
-            for k in (2, 3, 4, 5):
-                self.ring(dy, k).wait_recv()
+            came = pv.at[self.q, dy]
+            pltpu.make_async_copy(came, came, rs_r.at[self.q, dy, 2]).wait()
             own = pq[self.q, dy, 0].astype(F32)
             return own + pv[self.q, dy, 0].astype(F32) + pv[self.q, dy, 1].astype(F32)
 
@@ -376,7 +376,7 @@
             dst = zf.at[self.sub, yd, side] if k < 2 else zr.at[yd, side, rows]
             return remote(
                 wq.at[self.half * N_T + j, rows], dst, z_s.at[self.sub],
-                z_r.at[self.sub, yd, k], dp=dev(0, step, 0),
+                z_r.at[self.sub, yd, min(k, 2)], dp=dev(0, step, 0),
             )
 
         def combine(self, *blocks):
@@ -495,9 +495,7 @@
     other = lax.rem(y_hi + 1, 2)
 
     def z_sum(yd, sub):
-        for k in (2, 3, 4, 5):
-            own = (q0, q2)[sub]
-            own.z_copy(yd * 4, k).wait_recv()
+        pltpu.make_async_copy(zr.at[yd, 0], zr.at[yd, 0], z_r.at[sub, yd, 2]).wait()
         rows = slice(sub * W, (sub + 1) * W)
         total = wq[core * N_T + yd * 4 + z, rows].astype(F32)
         return total + zr[yd, 0, rows].astype(F32) + zr[yd, 1, rows].astype(F32)
@@ -549,25 +547,25 @@
     q2.own_sum()
     q0.last()
     q1.far()
+    q3.finish()
     q1.next_use()
     q2.near()
+    q3.own()
     q1.far_use()
-    q3.finish()
-    q3.own()
     q2.near_use()
+    q2.far()
+    q3.near()
+    q3.own_sum()
     q0.relay_far()
-    q2.far()
-    q3.own_sum()
     q1.relay_near()
     q1.last_use()
     q0.relay_last()
-    q3.near()
     q2.next_use()
     q1.last()
     q2.far_use()
     q3.near_use()
+    q3.far()
     q1.relay_far()
-    q3.far()
     nrm_cross(3)
     q2.relay_near()
     q2.last_use()
@@ -606,7 +604,7 @@
     def gs_copy(ry, rz):
         b = dev(ry, 4 - rz, 0)
         return remote(
-            grd_g.at[b], grd_g.at[b], gs_s, gs_r.at[ry, rz], dp=dev(0, 0, 1)
+            grd_g.at[b], grd_g.at[b], gs_s, gs_r.at[ry], dp=dev(0, 0, 1)
         )
 
     def gz_copy(ry, k, sender=True):
@@ -624,7 +622,7 @@
     def hs_copy(ry, rz):
         b = dev(ry, 4 - rz, 0)
         return remote(
-            gkv_g.at[b], gkv_g.at[b], hs_s, hs_r.at[ry, rz], dp=dev(0, 0, 1)
+            gkv_g.at[b], gkv_g.at[b], hs_s, hs_r.at[ry], dp=dev(0, 0, 1)
         )
 
     def hz_copy(k, sender=True):
@@ -689,21 +687,9 @@
         return of_query, mm_tn(lhs, gkv_g[rows].reshape(N_T * SEQ, 2 * HD))
 
     def arrived(ry):
-        for rz in range(4):
-            for rc in range(2):
-                if (ry, rz, rc) != (0, 0, 0):
-                    src = dev(ry, 4 - rz, rc)
-                    r = (ry * 4 + rz) * 2 + rc
-                    remote(
-                        nrm_g.at[src], nrm_g.at[src], nrm_s, nrm_r.at[r], dp=src
-                    ).wait_recv()
-            b = dev(ry, 4 - rz, 1)
-            remote(
-                grd_g.at[b], grd_g.at[b], gs_s, gs_r.at[ry, rz], dp=dev(0, 0, 1)
-            ).wait_recv()
-            remote(
-                gkv_g.at[b], gkv_g.at[b], hs_s, hs_r.at[ry, rz], dp=dev(0, 0, 1)
-            ).wait_recv()
+        for ref, blocks, sem in ((nrm_g, N_T - 1 + ry, nrm_r), (grd_g, 4, gs_r), (gkv_g, 4, hs_r)):
+            came = ref.at[pl.ds(0, blocks)]
+            pltpu.make_async_copy(came, came, sem.at[ry]).wait()
 
     gz_copy(0, 2, False).wait_recv()
     gz_copy(0, 3, False).wait_recv()
@@ -825,9 +811,9 @@
         pltpu.VMEM((2 * HEADS * SEQ, HD), BF16),
         pltpu.VMEM((4, SEQ, HD), BF16),
         dma((2,)), dma((4,)), dma((3, 4)), dma,
-        dma, dma((N_DP,)), dma((2,)), dma((N_T, 2)), dma((2,)), dma((2, 2, 6)), dma((2,)), dma((2,)),
-        dma, dma((2, 4)), dma, dma, dma((2, 4)), dma, dma((4,)), dma((4,)), dma, dma((2, 4)),
-        dma((4,)), dma((4, 2, 6)), dma((7,)), dma((4,)), dma((4, 9)),
+        dma, dma((2,)), dma((2,)), dma((N_T, 2)), dma((2,)), dma((2, 2, 3)), dma((2,)), dma((2,)),
+        dma, dma((2, 4)), dma, dma, dma((2,)), dma, dma((4,)), dma((4,)), dma, dma((2,)),
+        dma((4,)), dma((4, 2, 3)), dma((7,)), dma((4,)), dma((4, 9)),
     ]
     shapes = tuple(jax.ShapeDtypeStruct((C, n), F32) for n in (QW, HD, HD, QW))
     results = pl.pallas_call(

time: 116 us -> 116 us (level)
  no operation moved by 1% of the time
where the time goes in v6:
time: 116 us
  Pallas kernels  115 us (99%)
    pallas_call x1, Pallas kernels, local(): pl.pallas_call(kernel, out_shape=shapes, in_specs=[any_spec, any_spec, vm...  112 us
    pallas_call x1, Pallas kernels, local(): pl.pallas_call(hand_over, out_shape=shapes, in_specs=[any_spec] * 4, out_...  2.66 us

profile of v6, /device:TPU:13, one launch (start us, length us, event | category | flops | bytes accessed | tf_op | source)
XLA Modules:
  0.0 115.7 jit_solution(9534892779337607636)
XLA Ops:
  0.6 112.2 %hvp.1 = (f32[512,512]{1,0:T(8,128)}, f32[512,128]{1,0:T(8,128)}, f32[512,128]{1,0:T(8,128)}, f32[512,512]{1,0:T(8,128)}) custom-call(bf16[128,8192]{1,0:T(8,128)(2,1)} %tok_hbm.1, bf16[128,8192]{1,0:T(8,128)(2,1)} %tgt_hbm.1, f32[1,8192]{1,0:T(1,128)} %bitcast.11, bf16[16,512,512]{2,1,0:T(8,128)(2,1)} %bitcast.8, bf16[16,512,128]{2,1,0:T(8,128)(2,1)} %bitcast.9, ...), custom_call_target="tpu_custom_call" | custom-call | flops 10000000000 | bytes 26000000 | tf_op jit(solution)/shard_map/hvp/pallas_call | solution.py:819
  112.9 2.7 %results.1 = (f32[512,512]{1,0:T(8,128)}, f32[512,128]{1,0:T(8,128)}, f32[512,128]{1,0:T(8,128)}, f32[512,512]{1,0:T(8,128)}) custom-call(f32[512,512]{1,0:T(8,128)} %get-tuple-element.8.a, f32[512,128]{1,0:T(8,128)} %get-tuple-element.9.b, f32[512,128]{1,0:T(8,128)} %get-tuple-element.10.c, f32[512,512]{1,0:T(8,128)} %get-tuple-element.11.e), custom_call_target="tpu_custom_call" | custom-call | tf_op jit(solution)/shard_map/results/pallas_call | solution.py:841

commit v7 on v6

--- a/solution.py
+++ b/solution.py
@@ -572,7 +572,6 @@
     q3.next_use()
     q2.last()
     q1.relay_last()
-    out_cross(0)
     q3.far_use()
     q3.last_use()
 
@@ -653,6 +652,7 @@
     hs_copy(0, 0).start()
     gs_copy(0, 0).start()
     q3.relay_near()
+    out_cross(0)
     q3.last()
     q2.relay_far()
     q2.relay_last()

time: 116 us -> 116 us (level)
  no operation moved by 1% of the time
where the time goes in v7:
time: 116 us
  Pallas kernels  115 us (99%)
    pallas_call x1, Pallas kernels, local(): pl.pallas_call(kernel, out_shape=shapes, in_specs=[any_spec, any_spec, vm...  112 us
    pallas_call x1, Pallas kernels, local(): pl.pallas_call(hand_over, out_shape=shapes, in_specs=[any_spec] * 4, out_...  2.66 us

profile of v7, /device:TPU:13, one launch (start us, length us, event | category | flops | bytes accessed | tf_op | source)
XLA Modules:
  0.0 115.7 jit_solution(3856131299275472757)
XLA Ops:
  0.6 112.2 %hvp.1 = (f32[512,512]{1,0:T(8,128)}, f32[512,128]{1,0:T(8,128)}, f32[512,128]{1,0:T(8,128)}, f32[512,512]{1,0:T(8,128)}) custom-call(bf16[128,8192]{1,0:T(8,128)(2,1)} %tok_hbm.1, bf16[128,8192]{1,0:T(8,128)(2,1)} %tgt_hbm.1, f32[1,8192]{1,0:T(1,128)} %bitcast.11, bf16[16,512,512]{2,1,0:T(8,128)(2,1)} %bitcast.8, bf16[16,512,128]{2,1,0:T(8,128)(2,1)} %bitcast.9, ...), custom_call_target="tpu_custom_call" | custom-call | flops 10000000000 | bytes 26000000 | tf_op jit(solution)/shard_map/hvp/pallas_call | solution.py:819
  112.9 2.7 %results.1 = (f32[512,512]{1,0:T(8,128)}, f32[512,128]{1,0:T(8,128)}, f32[512,128]{1,0:T(8,128)}, f32[512,512]{1,0:T(8,128)}) custom-call(f32[512,512]{1,0:T(8,128)} %get-tuple-element.8.a, f32[512,128]{1,0:T(8,128)} %get-tuple-element.9.b, f32[512,128]{1,0:T(8,128)} %get-tuple-element.10.c, f32[512,512]{1,0:T(8,128)} %get-tuple-element.11.e), custom_call_target="tpu_custom_call" | custom-call | tf_op jit(solution)/shard_map/results/pallas_call | solution.py:841
